TPU v7x, 256 devices: a whole 4x4x8 slice. The times are simulated.
256 devices in a mesh: row: 32 (over z, y), col: 8 (over x, core).
Axes of the slice: x: 4, y: 4, z: 8, core: 2. Of those that a mesh axis runs over, the one named last changes fastest.
Arguments:
- head_deflections: float32 [256, 3, 2, 1024], P('row', None, None, 'col'), may hold values from -6 to 6
- diag_inverse: float32 [2, 1024, 1024], P(None, None, 'col'), may hold values from -1 to 2, as said below
- coupling: float32 [1024, 1024], P(None, 'col'), may hold values from -0.1875 to 0.1875
- panel_factor: float32 [32768, 2, 1024], P('row', None, 'col'), may hold values from -0.125 to 0.125
- trailing: float32 [256, 3, 32768], P('col', None, 'row'), may hold values from -6 to 6
Outputs:
- solved: float32 [256, 3, 2, 1024], P('row', None, None, 'col')
- rest: float32 [256, 3, 32768], P('col', None, 'row')
Inputs may be any that keep to these rules, and one draw needn't show every extreme that they name: Each diag_inverse[p] is lower triangular with a positive diagonal.
All inputs are finite; a program needn't handle non-finite values.
Results may differ from a plain program's by a relative error of at most 0.00007.
Values sent between devices are 32-bit elements; how exact they have to be, the bound alone decides.
A program may use at most 64 MiB of HBM per device.

v0:
```python
import jax
import jax.numpy as jnp
from jax import lax
from jax.sharding import PartitionSpec as P


def apply_cols(matrix, vectors):
    return lax.dot_general(
        vectors,
        matrix,
        (((2,), (1,)), ((), ())),
        precision=lax.Precision.HIGHEST,
        preferred_element_type=jnp.float32,
    )


def solve_first(block_rhs, diag_inverse):
    return lax.psum_scatter(
        apply_cols(diag_inverse[0], block_rhs), "col", scatter_dimension=2, tiled=True
    )


def solve_second(block_rhs, first_solved, diag_inverse, coupling):
    moved = lax.psum_scatter(
        apply_cols(coupling, first_solved), "col", scatter_dimension=2, tiled=True
    )
    carried = block_rhs - moved
    return lax.psum_scatter(
        apply_cols(diag_inverse[1], carried), "col", scatter_dimension=2, tiled=True
    )


def share_steps(solved_own):
    return lax.all_gather(solved_own, "row", axis=0, tiled=True)


def panel_terms(solved_all, factor):
    return lax.dot_general(
        solved_all,
        factor,
        (((2,), (1,)), ((), ())),
        precision=lax.Precision.HIGHEST,
        preferred_element_type=jnp.float32,
    )


def panel_update(solved_all, factor):
    return lax.psum_scatter(panel_terms(solved_all, factor), "col", scatter_dimension=0, tiled=True)


def body(head_deflections, diag_inverse, coupling, panel_factor, trailing):
    first_own = solve_first(head_deflections[:, :, 0, :], diag_inverse)
    first_all = share_steps(first_own)
    first_update = panel_update(first_all, panel_factor[:, 0, :])
    second_own = solve_second(head_deflections[:, :, 1, :], first_own, diag_inverse, coupling)
    second_all = share_steps(second_own)
    rest = trailing - first_update - panel_update(second_all, panel_factor[:, 1, :])
    solved = jnp.stack([first_own, second_own], axis=2)
    return (solved, rest)


def solution(mesh):
    placed = (
        P("row", None, None, "col"),
        P(None, None, "col"),
        P(None, "col"),
        P("row", None, "col"),
        P("col", None, "row"),
    )
    return jax.shard_map(
        body,
        mesh=mesh,
        in_specs=placed,
        out_specs=(P("row", None, None, "col"), P("col", None, "row")),
        check_vma=False,
    )
```

profile of v0, /device:TPU:38, one launch (start us, length us, event | category | flops | bytes accessed | tf_op | source)
XLA Modules:
  0.0 214.7 jit_solution(16585758415949704125)
XLA Ops:
  7.2 0.0 copy-start
  7.2 0.0 copy-start.1
  7.2 0.0 reduce-scatter.6.cloned.1.call-start
  7.2 0.9 fusion.11
  8.1 2.2 %fusion.4 = f32[8,3,1024]{2,0,1:T(8,128)} fusion(f32[2,1024,128]{2,1,0:T(8,128)} %param.6, f32[8,3,1,128]{3,2,1,0:T(1,128)S(1)} %get-tuple-element.9), kind=kOutput, calls=%fused_computation.4 | convolution fusion | flops 37748736 | bytes 634880 | tf_op jit(solution)/shard_map/dot_general | solution.py:8
  10.3 0.0 reduce-scatter.6.cloned.1.call-update
  10.4 0.0 reduce-scatter.8.cloned.1.call-start
  10.4 33.1 %reduce-scatter.6.cloned.1.call-done = f32[8,3,128]{2,0,1:T(8,128)} async-done(((f32[8,3,1024]{2,0,1:T(8,128)}), f32[8,3,128]{2,0,1:T(8,128)}) %reduce-scatter.6.cloned.1.call-update) | async-done | bytes 12304 | tf_op jit(solution)/shard_map/reduce_scatter | solution.py:18
  43.5 0.0 copy-done
  43.5 1.9 fusion.2
  45.4 0.0 reduce-scatter.8.cloned.1.call-update
  45.4 0.0 reduce-scatter.10.cloned.1.call-start
  45.5 2.5 %fusion.10 = (f32[1024,1,128]{2,1,0:T(1,128)S(1)}, f32[1024,1,128]{2,1,0:T(1,128)S(1)}) fusion(f32[1024,2,128]{2,1,0:T(2,128)} %param.8), kind=kLoop, calls=%fused_computation.13 | loop fusion | bytes 2097152 | tf_op jit(solution)/shard_map/slice | solution.py:54
  48.0 44.0 %all_gather.6 = f32[256,3,128]{2,0,1:T(8,128)S(1)} all-gather(f32[8,3,128]{2,0,1:T(8,128)} %reduce-scatter.6.cloned.1.call-done), channel_id=1, replica_groups=mesh['row'=32,'col'=8] {'row'}, dimensions={0}, use_global_device_ids=true | all-gather | bytes 405504 | tf_op jit(solution)/shard_map/all_gather | solution.py:34
  92.0 0.0 reduce-scatter.8.cloned.1.call-done
  92.0 0.0 copy-done.1
  92.0 1.9 fusion
  93.9 0.0 reduce-scatter.10.cloned.1.call-update
  93.9 0.0 reduce-scatter.12.cloned.1.call-start
  94.0 4.3 %fusion.12 = f32[256,3,1024]{2,0,1:T(8,128)} fusion(f32[256,3,128]{2,0,1:T(8,128)S(1)} %all_gather.6, f32[1024,128,1]{1,0,2:T(8,128)S(1)} %bitcast.35), kind=kOutput, calls=%fused_computation.15 | convolution fusion | flops 1207959552 | bytes 4063232 | tf_op jit(solution)/shard_map/dot_general | solution.py:38
  98.2 0.0 reduce-scatter.12.cloned.1.call-update
  98.3 0.0 reduce-scatter.14.cloned.1.call-start
  98.3 25.0 %reduce-scatter.10.cloned.1.call-done = f32[8,3,128]{2,0,1:T(8,128)} async-done(((f32[8,3,1024]{2,0,1:T(8,128)}), f32[8,3,128]{2,0,1:T(8,128)}) %reduce-scatter.10.cloned.1.call-update) | async-done | bytes 12304 | tf_op jit(solution)/shard_map/reduce_scatter | solution.py:28
  123.3 43.8 %all_gather.7 = f32[256,3,128]{2,0,1:T(8,128)S(1)} all-gather(f32[8,3,128]{2,0,1:T(8,128)} %reduce-scatter.10.cloned.1.call-done), channel_id=1, replica_groups=mesh['row'=32,'col'=8] {'row'}, dimensions={0}, use_global_device_ids=true | all-gather | bytes 405504 | tf_op jit(solution)/shard_map/all_gather | solution.py:34
  167.1 0.0 copy-start.3
  167.1 0.0 copy-start.4
  167.1 0.0 copy-start.2
  167.1 4.3 %fusion.13 = f32[256,3,1024]{2,0,1:T(8,128)} fusion(f32[256,3,128]{2,0,1:T(8,128)S(1)} %all_gather.7, f32[1024,128,1]{1,0,2:T(8,128)S(1)} %bitcast.34), kind=kOutput, calls=%fused_computation.16 | convolution fusion | flops 1207959552 | bytes 4063232 | tf_op jit(solution)/shard_map/dot_general | solution.py:38
  171.4 0.0 reduce-scatter.14.cloned.1.call-update
  171.4 0.0 copy-done.3
  171.4 0.0 copy-done.4
  171.4 0.6 copy.16
  172.1 0.0 reduce-scatter.12.cloned.1.call-done
  172.1 34.2 %reduce-scatter.14.cloned.1.call-done = f32[32,3,1024]{2,0,1:T(8,128)} async-done(((f32[256,3,1024]{2,0,1:T(8,128)}), f32[32,3,1024]{2,0,1:T(8,128)}) %reduce-scatter.14.cloned.1.call-update) | async-done | bytes 393232 | tf_op jit(solution)/shard_map/reduce_scatter | solution.py:48
  206.2 0.0 copy-done.2
  206.2 1.9 subtract_subtract_fusion
  (1 shorter events, 0.0 us)
Async XLA Ops:
  7.2 36.4 %copy-start = (f32[1024,128]{1,0:T(8,128)S(1)}, f32[1024,128]{1,0:T(8,128)}, u32[]{:S(2)}) copy-start(f32[1024,128]{1,0:T(8,128)} %param.7) | copy-start | bytes 1572868
  7.2 84.8 %copy-start.1 = (f32[2,1024,128]{2,1,0:T(8,128)S(1)}, f32[2,1024,128]{2,1,0:T(8,128)}, u32[]{:S(2)}) copy-start(f32[2,1024,128]{2,1,0:T(8,128)} %param.6) | copy-start | bytes 3145732
  7.2 36.3 %reduce-scatter.6.cloned.1.call-start = ((), (), s32[]{:S(2)}) async-start(), calls=%async_computation.5 | async-start | bytes 110592 | tf_op jit(solution)/shard_map/reduce_scatter | solution.py:18
  10.4 81.6 %reduce-scatter.8.cloned.1.call-start = ((), (), s32[]{:S(2)}) async-start(), calls=%async_computation.6 | async-start | bytes 110592 | tf_op jit(solution)/shard_map/reduce_scatter | solution.py:24
  45.4 77.8 %reduce-scatter.10.cloned.1.call-start = ((), (), s32[]{:S(2)}) async-start(), calls=%async_computation.7 | async-start | bytes 110592 | tf_op jit(solution)/shard_map/reduce_scatter | solution.py:28
  93.9 78.1 %reduce-scatter.12.cloned.1.call-start = ((), (), s32[]{:S(2)}) async-start(), calls=%async_computation.8 | async-start | bytes 3538944 | tf_op jit(solution)/shard_map/reduce_scatter | solution.py:48
  98.3 108.0 %reduce-scatter.14.cloned.1.call-start = ((), (), s32[]{:S(2)}) async-start(), calls=%async_computation.9 | async-start | bytes 3538944 | tf_op jit(solution)/shard_map/reduce_scatter | solution.py:48
  167.1 4.3 %copy-start.3 = (f32[8,3,128]{2,0,1:T(8,128)S(1)}, f32[8,3,128]{2,0,1:T(8,128)}, u32[]{:S(2)}) copy-start(f32[8,3,128]{2,0,1:T(8,128)} %reduce-scatter.6.cloned.1.call-done) | copy-start | bytes 36868
  167.1 4.3 %copy-start.4 = (f32[8,3,128]{2,0,1:T(8,128)S(1)}, f32[8,3,128]{2,0,1:T(8,128)}, u32[]{:S(2)}) copy-start(f32[8,3,128]{2,0,1:T(8,128)} %reduce-scatter.10.cloned.1.call-done) | copy-start | bytes 36868
  167.1 39.2 %copy-start.2 = (f32[32,3,1024]{2,0,1:T(8,128)S(1)}, f32[32,3,1024]{2,0,1:T(8,128)}, u32[]{:S(2)}) copy-start(f32[32,3,1024]{2,0,1:T(8,128)} %param.9) | copy-start | bytes 1179652
Sparse Core Ops, SparseCore 0:
  11.1 32.3 reduce-scatter.5
  46.7 31.7 reduce-scatter.7
  94.0 29.1 reduce-scatter.9
  125.8 36.7 reduce-scatter.11
  171.5 34.6 reduce-scatter.13
where the time goes:
time: 219 us; the launch traced here: 215 us
  waiting for transfers between devices  92.3 us (42%)
  blocking collectives  87.8 us (40%)
  matrix products  14.5 us (7%)
  between operations  13.8 us (6%)
  local copies, waits for them, and re-layouts  4.08 us (2%)
    all_gather x2, blocking collectives, share_steps(): return lax.all_gather(solved_own, 'row', axis=0, tiled=True)  87.8 us
    reduce_scatter x2, waiting for transfers between devices, panel_update(): lax.psum_scatter(panel_terms(solved_all, factor), 'col', scatter_dimensio...  34.2 us
    reduce_scatter x1, waiting for transfers between devices, solve_first(): lax.psum_scatter(apply_cols(diag_inverse[0], block_rhs), 'col', scatter_d...  33.1 us
    reduce_scatter x1, waiting for transfers between devices, solve_second(): lax.psum_scatter(apply_cols(diag_inverse[1], carried), 'col', scatter_dim...  25 us
    dot_general x2, matrix products, panel_terms(): lax.dot_general(solved_all, factor, (((2,), (1,)), ((), ())), precision=l...  8.56 us
    dot_general x3, matrix products, apply_cols(): lax.dot_general(vectors, matrix, (((2,), (1,)), ((), ())), precision=lax....  5.98 us
  transfers between devices with their start and end apart: 5, of which 3 were waited for; matrix products, arithmetic and copies ran while one was open for 5% of the time, Pallas kernels for 0%

commit v1 on v0

v1 whole, which is shorter than its diff:
```python
import functools

import jax
import jax.numpy as jnp
from jax import lax
from jax.experimental import pallas as pl
from jax.experimental.pallas import tpu as pltpu
from jax.sharding import PartitionSpec as P

MESH = pl.DeviceIdType.MESH
F32 = jnp.float32
BF16 = jnp.bfloat16
NX, NY, NZ = 4, 4, 8
NC = 8
V = 24
W = 128
HALF = 512
LAG = 3
NT = (((1,), (1,)), ((), ()))


def split(value):
    high = value.astype(BF16)
    return high, (value - high.astype(F32)).astype(BF16)


def kernel(h_ref, d_ref, c_ref, f_ref, sol_ref, upd_ref,
           d_buf, c_buf, f_buf, ft_hi, ft_lo, part, got, S, acc, M, R, L,
           load_sem, fs, fr, a_ss, a_rs, y_ss, y_rs, z_ss, z_rs, p_ss, p_rs, e_ss, e_rs):
    row, col = lax.axis_index("row"), lax.axis_index("col")
    z, y = row // NY, row % NY
    x, k = col // 2, col % 2
    step_k = 1 - 2 * k
    mate = x * 2 + 1 - k
    next_z = (z + step_k + NZ) % NZ
    prev_z = (z - step_k + NZ) % NZ

    def place(zz, yy):
        return zz * NY + yy

    def remote(src, dst, ss, rs, to):
        return pltpu.make_async_remote_copy(
            src_ref=src, dst_ref=dst, send_sem=ss, recv_sem=rs, device_id=to, device_id_type=MESH)

    partner = (row, mate)
    ring_to = (place(next_z, y), col)

    barrier = pltpu.get_barrier_semaphore()
    friends = [(row, (col + o) % NC) for o in range(1, NC)]
    y_list = [(dy, dk) for dy in range(NY) for dk in range(2) if (dy, dk) != (0, 0)]
    y_dev = [(place(z, (y + dy) % NY), x * 2 + (k + dk) % 2) for dy, dk in y_list]
    friends += [dev for (dy, dk), dev in zip(y_list, y_dev) if dy]
    friends += [ring_to, (place(prev_z, y), col)]
    for dev in friends:
        pl.semaphore_signal(barrier, inc=1, device_id=dev, device_id_type=MESH)

    loads = [
        pltpu.make_async_copy(d_ref.at[0], d_buf.at[0], load_sem.at[0]),
        pltpu.make_async_copy(c_ref, c_buf, load_sem.at[1]),
        pltpu.make_async_copy(d_ref.at[1], d_buf.at[1], load_sem.at[2]),
    ]
    mine = pl.ds(pl.multiple_of(k * HALF, HALF), HALF)
    theirs = pl.ds(pl.multiple_of((1 - k) * HALF, HALF), HALF)
    for p in range(2):
        loads.append(pltpu.make_async_copy(f_ref.at[mine, p], f_buf.at[p, k], load_sem.at[3 + p]))
    for load in loads:
        load.start()

    def partial(stage, value, matrix):
        hi, lo = split(value)
        both = jnp.concatenate([hi, lo], axis=0)
        for b in range(NC):
            m_hi, m_lo = split(matrix[b * W:(b + 1) * W, :])
            one = lax.dot_general(both, m_hi, NT, preferred_element_type=F32)
            two = lax.dot_general(hi, m_lo, NT, preferred_element_type=F32)
            part[stage, b] = one[:V] + (one[V:] + two)

    def exchange(stage):
        copies = []
        for o in range(1, NC):
            to = (col + o) % NC
            copies.append(remote(part.at[stage, to], got.at[stage, o], a_ss.at[stage, o], a_rs.at[stage, o], (row, to)))
        for copy in copies:
            copy.start()
        return copies

    def collect(stage, copies):
        total = part[stage, col]
        for o in range(1, NC):
            copies[o - 1].wait_recv()
            total = total + got[stage, o]
        return total

    def share(p):
        copies = []
        for i, dev in enumerate(y_dev):
            here = S.at[p, z, k, y]
            copies.append(remote(here, here, y_ss.at[p, i], y_rs.at[p, i], dev))
        for copy in copies:
            copy.start()
        return copies

    def chunk(i):
        t = (i + 1) // 2
        sign = jnp.where(i % 2 == 1, -step_k, step_k)
        return (z + sign * t + NZ) % NZ

    def ring_send(p, t, c):
        return remote(S.at[p, c], S.at[p, c], z_ss.at[p, t], z_rs.at[p, t], ring_to)

    def ring_send_part(p, c):
        return remote(S.at[p, c, k], S.at[p, c, k], z_ss.at[p, 4], z_rs.at[p, 4], ring_to)

    def mate_send(p, t, c):
        return remote(S.at[p, c], S.at[p, c], p_ss.at[p, t], p_rs.at[p, t], partner)

    def mate_send_part(p, c):
        return remote(S.at[p, c, k], S.at[p, c, k], p_ss.at[p, 4], p_rs.at[p, 4], partner)

    def arrive(p, i):
        t = (i + 1) // 2
        c = chunk(i)

        @pl.when((i % 2 == 1) & (i < 7))
        def _():
            ring_send(p, t, c).wait_recv()

            @pl.when(i < 5)
            def _():
                ring_send(p, t + 1, c).start()

            @pl.when(i == 5)
            def _():
                ring_send_part(p, c).start()

            mate_send(p, t, c).start()

        @pl.when((i % 2 == 0) & (i > 0))
        def _():
            mate_send(p, t, c).wait_recv()

        @pl.when(i == 7)
        def _():
            ring_send_part(p, c).wait_recv()
            mate_send_part(p, c).start()
            mate_send_part(p, c).wait_recv()

    def update(p, c):
        s = jnp.concatenate([S[p, c, 0].reshape(4 * V, W), S[p, c, 1].reshape(4 * V, W)], axis=1)
        hi, lo = split(s)
        one = jnp.dot(jnp.concatenate([hi, lo], axis=0), ft_hi[p], preferred_element_type=F32)
        two = jnp.dot(hi, ft_lo[p], preferred_element_type=F32)
        return one[:4 * V] + (one[4 * V:] + two)

    loads[0].wait()
    partial(0, h_ref[0], d_buf.at[0])
    pl.semaphore_wait(barrier, len(friends))
    sent0 = exchange(0)
    f_sends = [remote(f_ref.at[theirs, p], f_buf.at[p, k], fs.at[p], fr.at[p], partner) for p in range(2)]
    for copy in f_sends:
        copy.start()
    loads[1].wait()
    loads[2].wait()
    first = collect(0, sent0)
    sol_ref[0] = first
    S[0, z, k, y] = first
    partial(1, first, c_buf)
    sent1 = exchange(1)
    shared0 = share(0)

    for p in range(2):
        loads[3 + p].wait()
        f_sends[p].wait_recv()
        for kk in range(2):
            hi, lo = split(f_buf[p, kk].T)
            ft_hi[p, kk * W:(kk + 1) * W, :] = hi
            ft_lo[p, kk * W:(kk + 1) * W, :] = lo

    carried = h_ref[1] - collect(1, sent1)
    partial(2, carried, d_buf.at[1])
    sent2 = exchange(2)
    for copy in shared0:
        copy.wait_recv()
    ring_send(0, 1, z).start()
    acc[z] = update(0, z)
    second = collect(2, sent2)
    sol_ref[1] = second
    S[1, z, k, y] = second
    shared1 = share(1)

    def first_loop(i, carry):
        arrive(0, i)
        c = chunk(i)
        acc[c] = update(0, c)
        return carry

    lax.fori_loop(1, 8, first_loop, 0)
    for copy in shared1:
        copy.wait_recv()
    ring_send(1, 1, z).start()

    up = (x + step_k + NX) % NX
    down = (x - step_k + NX) % NX

    def over(cc, c):
        return remote(acc.at[c], M.at[cc], e_ss.at[0, cc], e_rs.at[0, cc], (row, up * 2 + k))

    def merged(cc, c):
        return remote(acc.at[c], R.at[0, k], e_ss.at[1, cc], e_rs.at[1, k], (row, up * 2 + cc))

    def direct(cc, c):
        return remote(acc.at[c], R.at[1, k], e_ss.at[2, cc], e_rs.at[2, k], (row, down * 2 + cc))

    def local(c):
        return remote(acc.at[c], L.at[k], e_ss.at[3, 0], e_rs.at[3, 0], partner)

    def merge(i):
        c = chunk(i)
        cc = c % 2

        @pl.when(c // 2 == up)
        def _():
            over(cc, c).wait_recv()
            acc[c] = acc[c] + M[cc]
            merged(cc, c).start()

    def second_loop(i, carry):
        arrive(1, i)
        c = chunk(i)
        acc[c] = acc[c] + update(1, c)
        to, cc = c // 2, c % 2

        @pl.when((to != up) & (to != down) & (to != x))
        def _():
            over(cc, c).start()

        @pl.when(to == down)
        def _():
            direct(cc, c).start()

        @pl.when((to == x) & (cc != k))
        def _():
            local(c).start()

        @pl.when((to == x) & (cc == k))
        def _():
            L[k] = acc[c]

        @pl.when(i >= LAG)
        def _():
            merge(i - LAG)

        return carry

    lax.fori_loop(0, 8, second_loop, 0)

    def last_loop(i, carry):
        merge(i)
        return carry

    lax.fori_loop(8 - LAG, 8, last_loop, 0)

    local(z).wait_recv()
    for kk in range(2):
        remote(acc.at[0], R.at[1, kk], e_ss.at[2, 0], e_rs.at[2, kk], partner).wait_recv()
        remote(acc.at[0], R.at[0, kk], e_ss.at[1, 0], e_rs.at[1, kk], partner).wait_recv()
        upd_ref[:, kk * HALF:(kk + 1) * HALF] = L[kk] + (R[0, kk] + R[1, kk])

    for copy in sent0 + sent1 + sent2 + shared0 + shared1 + f_sends:
        copy.wait_send()
    for p in range(2):
        for t in range(1, 4):
            ring_send(p, t, z).wait_send()
            mate_send(p, t, z).wait_send()
        ring_send_part(p, z).wait_send()
        mate_send_part(p, z).wait_send()
    for cc in range(2):
        over(cc, z).wait_send()
        merged(cc, z).wait_send()
        direct(cc, z).wait_send()
    local(z).wait_send()


def body(head_deflections, diag_inverse, coupling, panel_factor, trailing):
    h = jnp.transpose(head_deflections.reshape(V, 2, W), (1, 0, 2))
    rows = panel_factor.shape[0]
    any_spec = pl.BlockSpec(memory_space=pl.ANY)
    vmem = pl.BlockSpec(memory_space=pltpu.VMEM)
    dma = pltpu.SemaphoreType.DMA
    solved, moved = pl.pallas_call(
        kernel,
        out_shape=(
            jax.ShapeDtypeStruct((2, V, W), F32),
            jax.ShapeDtypeStruct((4 * V, rows), F32),
        ),
        in_specs=[vmem, any_spec, any_spec, any_spec],
        out_specs=(vmem, vmem),
        scratch_shapes=[
            pltpu.VMEM((2, 1024, W), F32),
            pltpu.VMEM((1024, W), F32),
            pltpu.VMEM((2, 2, HALF, W), F32),
            pltpu.VMEM((2, 2 * W, HALF), BF16),
            pltpu.VMEM((2, 2 * W, HALF), BF16),
            pltpu.VMEM((3, NC, V, W), F32),
            pltpu.VMEM((3, NC, V, W), F32),
            pltpu.VMEM((2, NZ, 2, NY, V, W), F32),
            pltpu.VMEM((NC, 4 * V, HALF), F32),
            pltpu.VMEM((2, 4 * V, HALF), F32),
            pltpu.VMEM((2, 2, 4 * V, HALF), F32),
            pltpu.VMEM((2, 4 * V, HALF), F32),
            dma((5,)), dma((2,)), dma((2,)),
            dma((3, NC)), dma((3, NC)),
            dma((2, 7)), dma((2, 7)),
            dma((2, 5)), dma((2, 5)),
            dma((2, 5)), dma((2, 5)),
            dma((4, 2)), dma((4, 2)),
        ],
        compiler_params=pltpu.CompilerParams(
            collective_id=0, has_side_effects=True, vmem_limit_bytes=32 << 20),
    )(h, diag_inverse, coupling, panel_factor)
    rest = trailing - moved.reshape(trailing.shape)
    out = jnp.transpose(solved, (1, 0, 2)).reshape(head_deflections.shape)
    return (out, rest)


def solution(mesh):
    placed = (
        P("row", None, None, "col"),
        P(None, None, "col"),
        P(None, "col"),
        P("row", None, "col"),
        P("col", None, "row"),
    )
    return jax.shard_map(
        body,
        mesh=mesh,
        in_specs=placed,
        out_specs=(P("row", None, None, "col"), P("col", None, "row")),
        check_vma=False,
    )
```

time: 219 us -> 64.4 us (0.29)
  the two profiles are of different devices: /device:TPU:38 before, /device:TPU:37 now
where the time goes in v1:
time: 64.4 us; the launch traced here: 64.1 us
  Pallas kernels  56.3 us (87%)
  local copies, waits for them, and re-layouts  6.82 us (11%)
  between operations  0.65 us (1%)
    pallas_call x1, Pallas kernels, body(): pl.pallas_call(kernel, out_shape=(jax.ShapeDtypeStruct((2, V, W), F32), j...  56.3 us
    unnamed x9, local copies, waits for them, and re-layouts  5.3 us

profile of v1, /device:TPU:37, one launch (start us, length us, event | category | flops | bytes accessed | tf_op | source)
XLA Modules:
  0.0 64.1 jit_solution(2002809452699695878)
XLA Ops:
  0.6 0.7 %copy.16 = f32[24,2,128]{2,0,1:T(8,128)S(1)} copy(f32[24,2,128]{2,1,0:T(2,128)} %bitcast.8) | data formatting | bytes 49152 | tf_op jit(solution)/shard_map/reshape | solution.py:285
  1.4 0.0 copy-start
  1.4 1.2 %copy-done = f32[2,1024,128]{2,1,0:T(8,128)S(1)} copy-done((f32[2,1024,128]{2,1,0:T(8,128)S(1)}, f32[2,1024,128]{2,1,0:T(8,128)}, u32[]{:S(2)}) %copy-start) | copy-done | bytes 1048600
  2.6 0.0 copy-start.1
  2.6 1.2 %copy-done.1 = f32[1024,2,128]{2,1,0:T(2,128)S(1)} copy-done((f32[1024,2,128]{2,1,0:T(2,128)S(1)}, f32[1024,2,128]{2,1,0:T(2,128)}, u32[]{:S(2)}) %copy-start.1) | copy-done | bytes 1048600
  3.8 0.0 copy-start.2
  3.8 1.0 %copy-done.2 = f32[1024,128]{1,0:T(8,128)S(1)} copy-done((f32[1024,128]{1,0:T(8,128)S(1)}, f32[1024,128]{1,0:T(8,128)}, u32[]{:S(2)}) %copy-start.2) | copy-done | bytes 524312
  4.9 56.3 %shard_map.68 = (f32[2,24,128]{2,1,0:T(8,128)S(1)}, f32[96,1024]{1,0:T(8,128)S(1)}) custom-call(f32[2,24,128]{2,1,0:T(8,128)S(1)} %bitcast.6, f32[2,1024,128]{2,1,0:T(8,128)S(1)} %copy-done, f32[1024,128]{1,0:T(8,128)S(1)} %copy-done.2, f32[1024,2,128]{2,1,0:T(2,128)S(1)} %copy-done.1), custom_call_target="tpu_custom_call" | custom-call | tf_op jit(solution)/shard_map/pallas_call | solution.py:290
  61.2 0.6 copy.11
  61.8 0.0 copy-start.3
  61.8 0.2 reshape.15
  62.0 0.8 %copy-done.3 = f32[32,3,1024]{2,0,1:T(8,128)S(1)} copy-done((f32[32,3,1024]{2,0,1:T(8,128)S(1)}, f32[32,3,1024]{2,0,1:T(8,128)}, u32[]{:S(2)}) %copy-start.3) | copy-done | bytes 393240
  62.8 0.3 copy_subtract_fusion
  63.1 1.0 %copy.13 = f32[32,3,1024]{2,0,1:T(8,128)} copy(f32[32,3,1024]{2,1,0:T(4,128)S(1)} %copy_subtract_fusion) | data formatting | bytes 786432
Async XLA Ops:
  1.4 1.2 %copy-start = (f32[2,1024,128]{2,1,0:T(8,128)S(1)}, f32[2,1024,128]{2,1,0:T(8,128)}, u32[]{:S(2)}) copy-start(f32[2,1024,128]{2,1,0:T(8,128)} %d_ref.1) | copy-start | bytes 3145732
  2.6 1.2 %copy-start.1 = (f32[1024,2,128]{2,1,0:T(2,128)S(1)}, f32[1024,2,128]{2,1,0:T(2,128)}, u32[]{:S(2)}) copy-start(f32[1024,2,128]{2,1,0:T(2,128)} %f_ref.1) | copy-start | bytes 3145732
  3.8 1.0 %copy-start.2 = (f32[1024,128]{1,0:T(8,128)S(1)}, f32[1024,128]{1,0:T(8,128)}, u32[]{:S(2)}) copy-start(f32[1024,128]{1,0:T(8,128)} %c_ref.1) | copy-start | bytes 1572868
  61.8 1.0 %copy-start.3 = (f32[32,3,1024]{2,0,1:T(8,128)S(1)}, f32[32,3,1024]{2,0,1:T(8,128)}, u32[]{:S(2)}) copy-start(f32[32,3,1024]{2,0,1:T(8,128)} %param.9) | copy-start | bytes 1179652

commit v2 on v1

--- a/solution.py
+++ b/solution.py
@@ -25,8 +25,8 @@
 
 
 def kernel(h_ref, d_ref, c_ref, f_ref, sol_ref, upd_ref,
-           d_buf, c_buf, f_buf, ft_hi, ft_lo, part, got, S, acc, M, R, L,
-           load_sem, fs, fr, a_ss, a_rs, y_ss, y_rs, z_ss, z_rs, p_ss, p_rs, e_ss, e_rs):
+           h_buf, d_buf, c_buf, f_buf, ft_hi, ft_lo, part, got, S, acc, M, R, L,
+           h_sem, load_sem, fs, fr, a_ss, a_rs, y_ss, y_rs, z_ss, z_rs, p_ss, p_rs, e_ss, e_rs):
     row, col = lax.axis_index("row"), lax.axis_index("col")
     z, y = row // NY, row % NY
     x, k = col // 2, col % 2
@@ -63,7 +63,11 @@
     theirs = pl.ds(pl.multiple_of((1 - k) * HALF, HALF), HALF)
     for p in range(2):
         loads.append(pltpu.make_async_copy(f_ref.at[mine, p], f_buf.at[p, k], load_sem.at[3 + p]))
-    for load in loads:
+    heads = [
+        pltpu.make_async_copy(h_ref.at[:, comp, p], h_buf.at[p, comp * 8:(comp + 1) * 8], h_sem.at[p, comp])
+        for p in range(2) for comp in range(3)
+    ]
+    for load in heads + loads:
         load.start()
 
     def partial(stage, value, matrix):
@@ -152,8 +156,10 @@
         two = jnp.dot(hi, ft_lo[p], preferred_element_type=F32)
         return one[:4 * V] + (one[4 * V:] + two)
 
+    for load in heads:
+        load.wait()
     loads[0].wait()
-    partial(0, h_ref[0], d_buf.at[0])
+    partial(0, h_buf[0], d_buf.at[0])
     pl.semaphore_wait(barrier, len(friends))
     sent0 = exchange(0)
     f_sends = [remote(f_ref.at[theirs, p], f_buf.at[p, k], fs.at[p], fr.at[p], partner) for p in range(2)]
@@ -176,7 +182,7 @@
             ft_hi[p, kk * W:(kk + 1) * W, :] = hi
             ft_lo[p, kk * W:(kk + 1) * W, :] = lo
 
-    carried = h_ref[1] - collect(1, sent1)
+    carried = h_buf[1] - collect(1, sent1)
     partial(2, carried, d_buf.at[1])
     sent2 = exchange(2)
     for copy in shared0:
@@ -264,7 +270,11 @@
     for kk in range(2):
         remote(acc.at[0], R.at[1, kk], e_ss.at[2, 0], e_rs.at[2, kk], partner).wait_recv()
         remote(acc.at[0], R.at[0, kk], e_ss.at[1, 0], e_rs.at[1, kk], partner).wait_recv()
-        upd_ref[:, kk * HALF:(kk + 1) * HALF] = L[kk] + (R[0, kk] + R[1, kk])
+        moved = L[kk] + (R[0, kk] + R[1, kk])
+        for yy in range(NY):
+            for comp in range(3):
+                at = yy * V + comp * 8
+                upd_ref[comp, yy * 8:(yy + 1) * 8, kk * HALF:(kk + 1) * HALF] = moved[at:at + 8]
 
     for copy in sent0 + sent1 + sent2 + shared0 + shared1 + f_sends:
         copy.wait_send()
@@ -282,7 +292,6 @@
 
 
 def body(head_deflections, diag_inverse, coupling, panel_factor, trailing):
-    h = jnp.transpose(head_deflections.reshape(V, 2, W), (1, 0, 2))
     rows = panel_factor.shape[0]
     any_spec = pl.BlockSpec(memory_space=pl.ANY)
     vmem = pl.BlockSpec(memory_space=pltpu.VMEM)
@@ -291,11 +300,12 @@
         kernel,
         out_shape=(
             jax.ShapeDtypeStruct((2, V, W), F32),
-            jax.ShapeDtypeStruct((4 * V, rows), F32),
+            jax.ShapeDtypeStruct((3, 4 * 8, rows), F32),
         ),
-        in_specs=[vmem, any_spec, any_spec, any_spec],
+        in_specs=[any_spec] * 4,
         out_specs=(vmem, vmem),
         scratch_shapes=[
+            pltpu.VMEM((2, V, W), F32),
             pltpu.VMEM((2, 1024, W), F32),
             pltpu.VMEM((1024, W), F32),
             pltpu.VMEM((2, 2, HALF, W), F32),
@@ -308,7 +318,7 @@
             pltpu.VMEM((2, 4 * V, HALF), F32),
             pltpu.VMEM((2, 2, 4 * V, HALF), F32),
             pltpu.VMEM((2, 4 * V, HALF), F32),
-            dma((5,)), dma((2,)), dma((2,)),
+            dma((2, 3)), dma((5,)), dma((2,)), dma((2,)),
             dma((3, NC)), dma((3, NC)),
             dma((2, 7)), dma((2, 7)),
             dma((2, 5)), dma((2, 5)),
@@ -316,10 +326,10 @@
             dma((4, 2)), dma((4, 2)),
         ],
         compiler_params=pltpu.CompilerParams(
-            collective_id=0, has_side_effects=True, vmem_limit_bytes=32 << 20),
-    )(h, diag_inverse, coupling, panel_factor)
-    rest = trailing - moved.reshape(trailing.shape)
-    out = jnp.transpose(solved, (1, 0, 2)).reshape(head_deflections.shape)
+            collective_id=0, has_side_effects=True, vmem_limit_bytes=60 << 20),
+    )(head_deflections, diag_inverse, coupling, panel_factor)
+    rest = trailing - jnp.transpose(moved, (1, 0, 2))
+    out = jnp.transpose(solved.reshape(2, 3, 8, W), (2, 1, 0, 3))
     return (out, rest)
 
 

time: 64.4 us -> 61.2 us (0.950)
  local copies, waits for them, and re-layouts: 6.82 us -> 1.36 us
  other arithmetic: 0.34 us -> 1.78 us
  Pallas kernels: 56.3 us -> 57.2 us
    unnamed x9 -> x2, local copies, waits for them, and re-layouts: 5.3 us -> 0.01 us
    sub x1, other arithmetic: 0.34 us -> 1.78 us  [body(): rest = trailing - jnp.transpose(moved, (1, 0, 2))]
    pallas_call x1, Pallas kernels: 56.3 us -> 57.2 us  [body(): pl.pallas_call(kernel, out_shape=(jax.ShapeDtypeStruct((2, V, W), F32), j...]
    reshape x2 -> x1, local copies, waits for them, and re-layouts: 0.9 us -> 1.36 us  [body(): out = jnp.transpose(solved.reshape(2, 3, 8, W), (2, 1, 0, 3))]
where the time goes in v2:
time: 61.2 us; the launch traced here: 61 us
  Pallas kernels  57.2 us (93%)
  other arithmetic  1.78 us (3%)
  local copies, waits for them, and re-layouts  1.36 us (2%)
  between operations  0.65 us (1%)
    pallas_call x1, Pallas kernels, body(): pl.pallas_call(kernel, out_shape=(jax.ShapeDtypeStruct((2, V, W), F32), j...  57.2 us
    sub x1, other arithmetic, body(): rest = trailing - jnp.transpose(moved, (1, 0, 2))  1.78 us
    reshape x1, local copies, waits for them, and re-layouts, body(): out = jnp.transpose(solved.reshape(2, 3, 8, W), (2, 1, 0, 3))  1.36 us

profile of v2, /device:TPU:37, one launch (start us, length us, event | category | flops | bytes accessed | tf_op | source)
XLA Modules:
  0.0 61.0 jit_solution(14116483632129188835)
XLA Ops:
  0.6 0.0 copy-start
  0.6 57.2 %shard_map.68 = (f32[2,24,128]{2,1,0:T(8,128)}, f32[3,32,1024]{2,1,0:T(8,128)}) custom-call(f32[8,3,2,128]{3,2,1,0:T(2,128)} %h_ref.1, f32[2,1024,128]{2,1,0:T(8,128)} %d_ref.1, f32[1024,128]{1,0:T(8,128)} %c_ref.1, f32[1024,2,128]{2,1,0:T(2,128)} %f_ref.1), custom_call_target="tpu_custom_call" | custom-call | tf_op jit(solution)/shard_map/pallas_call | solution.py:299
  57.9 1.4 %copy.9 = f32[2,3,8,128]{3,0,1,2:T(2,128)} copy(f32[2,3,8,128]{3,2,1,0:T(8,128)} %bitcast.7) | data formatting | bytes 49152 | tf_op jit(solution)/shard_map/reshape | solution.py:332
  59.2 0.0 copy-done
  59.2 1.8 %bitcast_subtract_fusion = f32[32,3,1024]{2,0,1:T(8,128)} fusion(f32[32,3,1024]{2,0,1:T(8,128)S(1)} %copy-done, f32[3,32,1024]{2,1,0:T(8,128)} %get-tuple-element.5), kind=kLoop, calls=%fused_computation | loop fusion | flops 98304 | bytes 1179648 | tf_op jit(solution)/shard_map/sub | solution.py:331
Async XLA Ops:
  0.6 58.6 %copy-start = (f32[32,3,1024]{2,0,1:T(8,128)S(1)}, f32[32,3,1024]{2,0,1:T(8,128)}, u32[]{:S(2)}) copy-start(f32[32,3,1024]{2,0,1:T(8,128)} %param.9) | copy-start | bytes 1179652

commit v3 on v2

--- a/solution.py
+++ b/solution.py
@@ -15,7 +15,8 @@
 V = 24
 W = 128
 HALF = 512
-LAG = 3
+LAG = 4
+SPANS = (((0, 8),), ((0, 1), (1, 3), (3, 5), (5, 8)))
 NT = (((1,), (1,)), ((), ()))
 
 
@@ -26,14 +27,12 @@
 
 def kernel(h_ref, d_ref, c_ref, f_ref, sol_ref, upd_ref,
            h_buf, d_buf, c_buf, f_buf, ft_hi, ft_lo, part, got, S, acc, M, R, L,
-           h_sem, load_sem, fs, fr, a_ss, a_rs, y_ss, y_rs, z_ss, z_rs, p_ss, p_rs, e_ss, e_rs):
+           h_sem, load_sem, fs, fr, a_ss, a_rs, z_ss, z_rs, y_ss, y_rs, p_ss, p_rs, e_ss, e_rs):
     row, col = lax.axis_index("row"), lax.axis_index("col")
     z, y = row // NY, row % NY
     x, k = col // 2, col % 2
     step_k = 1 - 2 * k
     mate = x * 2 + 1 - k
-    next_z = (z + step_k + NZ) % NZ
-    prev_z = (z - step_k + NZ) % NZ
 
     def place(zz, yy):
         return zz * NY + yy
@@ -43,14 +42,11 @@
             src_ref=src, dst_ref=dst, send_sem=ss, recv_sem=rs, device_id=to, device_id_type=MESH)
 
     partner = (row, mate)
-    ring_to = (place(next_z, y), col)
 
     barrier = pltpu.get_barrier_semaphore()
     friends = [(row, (col + o) % NC) for o in range(1, NC)]
-    y_list = [(dy, dk) for dy in range(NY) for dk in range(2) if (dy, dk) != (0, 0)]
-    y_dev = [(place(z, (y + dy) % NY), x * 2 + (k + dk) % 2) for dy, dk in y_list]
-    friends += [dev for (dy, dk), dev in zip(y_list, y_dev) if dy]
-    friends += [ring_to, (place(prev_z, y), col)]
+    friends += [(place(z, (y + dy) % NY), col) for dy in range(1, NY)]
+    friends += [(place((z + dz) % NZ, y), col) for dz in range(1, NZ)]
     for dev in friends:
         pl.semaphore_signal(barrier, inc=1, device_id=dev, device_id_type=MESH)
 
@@ -95,59 +91,33 @@
             total = total + got[stage, o]
         return total
 
-    def share(p):
+    def share_z(p):
         copies = []
-        for i, dev in enumerate(y_dev):
-            here = S.at[p, z, k, y]
-            copies.append(remote(here, here, y_ss.at[p, i], y_rs.at[p, i], dev))
+        for i in range(1, NZ):
+            dz = (i + 1) // 2 if i % 2 == 1 else NZ - i // 2
+            there = (place((z + dz) % NZ, y), col)
+            copies.append(remote(S.at[p, 0, k, y], S.at[p, i, k, y], z_ss.at[p, i], z_rs.at[p, i], there))
         for copy in copies:
             copy.start()
         return copies
 
+    def share_y(p, n):
+        low, high = SPANS[p][n]
+        copies = []
+        for dy in range(1, NY):
+            block = S.at[p, pl.ds(low, high - low), k, y]
+            there = (place(z, (y + dy) % NY), col)
+            copies.append(remote(block, block, y_ss.at[p, n, dy], y_rs.at[p, n, dy], there))
+        return copies
+
+    def share_mate(p, n):
+        low, high = SPANS[p][n]
+        block = S.at[p, pl.ds(low, high - low), k]
+        return remote(block, block, p_ss.at[p, n], p_rs.at[p, n], partner)
+
     def chunk(i):
         t = (i + 1) // 2
-        sign = jnp.where(i % 2 == 1, -step_k, step_k)
-        return (z + sign * t + NZ) % NZ
-
-    def ring_send(p, t, c):
-        return remote(S.at[p, c], S.at[p, c], z_ss.at[p, t], z_rs.at[p, t], ring_to)
-
-    def ring_send_part(p, c):
-        return remote(S.at[p, c, k], S.at[p, c, k], z_ss.at[p, 4], z_rs.at[p, 4], ring_to)
-
-    def mate_send(p, t, c):
-        return remote(S.at[p, c], S.at[p, c], p_ss.at[p, t], p_rs.at[p, t], partner)
-
-    def mate_send_part(p, c):
-        return remote(S.at[p, c, k], S.at[p, c, k], p_ss.at[p, 4], p_rs.at[p, 4], partner)
-
-    def arrive(p, i):
-        t = (i + 1) // 2
-        c = chunk(i)
-
-        @pl.when((i % 2 == 1) & (i < 7))
-        def _():
-            ring_send(p, t, c).wait_recv()
-
-            @pl.when(i < 5)
-            def _():
-                ring_send(p, t + 1, c).start()
-
-            @pl.when(i == 5)
-            def _():
-                ring_send_part(p, c).start()
-
-            mate_send(p, t, c).start()
-
-        @pl.when((i % 2 == 0) & (i > 0))
-        def _():
-            mate_send(p, t, c).wait_recv()
-
-        @pl.when(i == 7)
-        def _():
-            ring_send_part(p, c).wait_recv()
-            mate_send_part(p, c).start()
-            mate_send_part(p, c).wait_recv()
+        return (z + jnp.where(i % 2 == 1, NZ - t, t)) % NZ
 
     def update(p, c):
         s = jnp.concatenate([S[p, c, 0].reshape(4 * V, W), S[p, c, 1].reshape(4 * V, W)], axis=1)
@@ -169,10 +139,10 @@
     loads[2].wait()
     first = collect(0, sent0)
     sol_ref[0] = first
-    S[0, z, k, y] = first
+    S[0, 0, k, y] = first
     partial(1, first, c_buf)
     sent1 = exchange(1)
-    shared0 = share(0)
+    z0_sent = share_z(0)
 
     for p in range(2):
         loads[3 + p].wait()
@@ -185,40 +155,47 @@
     carried = h_buf[1] - collect(1, sent1)
     partial(2, carried, d_buf.at[1])
     sent2 = exchange(2)
-    for copy in shared0:
+    for copy in z0_sent:
         copy.wait_recv()
-    ring_send(0, 1, z).start()
-    acc[z] = update(0, z)
+    for copy in share_y(0, 0):
+        copy.start()
     second = collect(2, sent2)
     sol_ref[1] = second
-    S[1, z, k, y] = second
-    shared1 = share(1)
+    S[1, 0, k, y] = second
+    spans = range(len(SPANS[1]))
+    for copy in share_y(1, 0):
+        copy.start()
+    z1_sent = share_z(1)
+    for copy in share_y(0, 0):
+        copy.wait_recv()
+    share_mate(0, 0).start()
+    for n in spans[1:]:
+        for i in range(*SPANS[1][n]):
+            z1_sent[i - 1].wait_recv()
+        for copy in share_y(1, n):
+            copy.start()
+    share_mate(0, 0).wait_recv()
 
     def first_loop(i, carry):
-        arrive(0, i)
-        c = chunk(i)
-        acc[c] = update(0, c)
+        acc[i] = update(0, i)
         return carry
 
-    lax.fori_loop(1, 8, first_loop, 0)
-    for copy in shared1:
-        copy.wait_recv()
-    ring_send(1, 1, z).start()
+    lax.fori_loop(0, 8, first_loop, 0)
 
     up = (x + step_k + NX) % NX
     down = (x - step_k + NX) % NX
 
-    def over(cc, c):
-        return remote(acc.at[c], M.at[cc], e_ss.at[0, cc], e_rs.at[0, cc], (row, up * 2 + k))
-
-    def merged(cc, c):
-        return remote(acc.at[c], R.at[0, k], e_ss.at[1, cc], e_rs.at[1, k], (row, up * 2 + cc))
-
-    def direct(cc, c):
-        return remote(acc.at[c], R.at[1, k], e_ss.at[2, cc], e_rs.at[2, k], (row, down * 2 + cc))
-
-    def local(c):
-        return remote(acc.at[c], L.at[k], e_ss.at[3, 0], e_rs.at[3, 0], partner)
+    def over(cc, i):
+        return remote(acc.at[i], M.at[cc], e_ss.at[0, cc], e_rs.at[0, cc], (row, up * 2 + k))
+
+    def merged(cc, i):
+        return remote(acc.at[i], R.at[0, k], e_ss.at[1, cc], e_rs.at[1, k], (row, up * 2 + cc))
+
+    def direct(cc, i):
+        return remote(acc.at[i], R.at[1, k], e_ss.at[2, cc], e_rs.at[2, k], (row, down * 2 + cc))
+
+    def local(i):
+        return remote(acc.at[i], L.at[k], e_ss.at[3, 0], e_rs.at[3, 0], partner)
 
     def merge(i):
         c = chunk(i)
@@ -226,31 +203,38 @@
 
         @pl.when(c // 2 == up)
         def _():
-            over(cc, c).wait_recv()
-            acc[c] = acc[c] + M[cc]
-            merged(cc, c).start()
+            over(cc, i).wait_recv()
+            acc[i] = acc[i] + M[cc]
+            merged(cc, i).start()
 
     def second_loop(i, carry):
-        arrive(1, i)
+        for n in spans:
+            @pl.when(i == SPANS[1][n][0])
+            def _():
+                for copy in share_y(1, n):
+                    copy.wait_recv()
+                share_mate(1, n).start()
+                share_mate(1, n).wait_recv()
+
         c = chunk(i)
-        acc[c] = acc[c] + update(1, c)
+        acc[i] = acc[i] + update(1, i)
         to, cc = c // 2, c % 2
 
         @pl.when((to != up) & (to != down) & (to != x))
         def _():
-            over(cc, c).start()
+            over(cc, i).start()
 
         @pl.when(to == down)
         def _():
-            direct(cc, c).start()
+            direct(cc, i).start()
 
         @pl.when((to == x) & (cc != k))
         def _():
-            local(c).start()
+            local(i).start()
 
         @pl.when((to == x) & (cc == k))
         def _():
-            L[k] = acc[c]
+            L[k] = acc[i]
 
         @pl.when(i >= LAG)
         def _():
@@ -266,7 +250,7 @@
 
     lax.fori_loop(8 - LAG, 8, last_loop, 0)
 
-    local(z).wait_recv()
+    local(0).wait_recv()
     for kk in range(2):
         remote(acc.at[0], R.at[1, kk], e_ss.at[2, 0], e_rs.at[2, kk], partner).wait_recv()
         remote(acc.at[0], R.at[0, kk], e_ss.at[1, 0], e_rs.at[1, kk], partner).wait_recv()
@@ -276,19 +260,18 @@
                 at = yy * V + comp * 8
                 upd_ref[comp, yy * 8:(yy + 1) * 8, kk * HALF:(kk + 1) * HALF] = moved[at:at + 8]
 
-    for copy in sent0 + sent1 + sent2 + shared0 + shared1 + f_sends:
+    for copy in sent0 + sent1 + sent2 + z0_sent + z1_sent + f_sends:
         copy.wait_send()
     for p in range(2):
-        for t in range(1, 4):
-            ring_send(p, t, z).wait_send()
-            mate_send(p, t, z).wait_send()
-        ring_send_part(p, z).wait_send()
-        mate_send_part(p, z).wait_send()
+        for n in range(len(SPANS[p])):
+            for copy in share_y(p, n):
+                copy.wait_send()
+            share_mate(p, n).wait_send()
     for cc in range(2):
-        over(cc, z).wait_send()
-        merged(cc, z).wait_send()
-        direct(cc, z).wait_send()
-    local(z).wait_send()
+        over(cc, 0).wait_send()
+        merged(cc, 0).wait_send()
+        direct(cc, 0).wait_send()
+    local(0).wait_send()
 
 
 def body(head_deflections, diag_inverse, coupling, panel_factor, trailing):
@@ -320,9 +303,9 @@
             pltpu.VMEM((2, 4 * V, HALF), F32),
             dma((2, 3)), dma((5,)), dma((2,)), dma((2,)),
             dma((3, NC)), dma((3, NC)),
-            dma((2, 7)), dma((2, 7)),
-            dma((2, 5)), dma((2, 5)),
-            dma((2, 5)), dma((2, 5)),
+            dma((2, NZ)), dma((2, NZ)),
+            dma((2, 4, NY)), dma((2, 4, NY)),
+            dma((2, 4)), dma((2, 4)),
             dma((4, 2)), dma((4, 2)),
         ],
         compiler_params=pltpu.CompilerParams(

time: 61.2 us -> 55.4 us (0.905)
  Pallas kernels: 57.2 us -> 51.4 us
    pallas_call x1, Pallas kernels: 57.2 us -> 51.4 us  [body(): pl.pallas_call(kernel, out_shape=(jax.ShapeDtypeStruct((2, V, W), F32), j...]
where the time goes in v3:
time: 55.4 us; the launch traced here: 55.2 us
  Pallas kernels  51.4 us (93%)
  other arithmetic  1.78 us (3%)
  local copies, waits for them, and re-layouts  1.36 us (2%)
  between operations  0.65 us (1%)
    pallas_call x1, Pallas kernels, body(): pl.pallas_call(kernel, out_shape=(jax.ShapeDtypeStruct((2, V, W), F32), j...  51.4 us
    sub x1, other arithmetic, body(): rest = trailing - jnp.transpose(moved, (1, 0, 2))  1.78 us
    reshape x1, local copies, waits for them, and re-layouts, body(): out = jnp.transpose(solved.reshape(2, 3, 8, W), (2, 1, 0, 3))  1.36 us

profile of v3, /device:TPU:37, one launch (start us, length us, event | category | flops | bytes accessed | tf_op | source)
XLA Modules:
  0.0 55.2 jit_solution(13504272941066904992)
XLA Ops:
  0.6 0.0 copy-start
  0.6 51.4 %shard_map.68 = (f32[2,24,128]{2,1,0:T(8,128)}, f32[3,32,1024]{2,1,0:T(8,128)}) custom-call(f32[8,3,2,128]{3,2,1,0:T(2,128)} %h_ref.1, f32[2,1024,128]{2,1,0:T(8,128)} %d_ref.1, f32[1024,128]{1,0:T(8,128)} %c_ref.1, f32[1024,2,128]{2,1,0:T(2,128)} %f_ref.1), custom_call_target="tpu_custom_call" | custom-call | tf_op jit(solution)/shard_map/pallas_call | solution.py:282
  52.1 1.4 %copy.9 = f32[2,3,8,128]{3,0,1,2:T(2,128)} copy(f32[2,3,8,128]{3,2,1,0:T(8,128)} %bitcast.7) | data formatting | bytes 49152 | tf_op jit(solution)/shard_map/reshape | solution.py:315
  53.5 0.0 copy-done
  53.5 1.8 %bitcast_subtract_fusion = f32[32,3,1024]{2,0,1:T(8,128)} fusion(f32[32,3,1024]{2,0,1:T(8,128)S(1)} %copy-done, f32[3,32,1024]{2,1,0:T(8,128)} %get-tuple-element.5), kind=kLoop, calls=%fused_computation | loop fusion | flops 98304 | bytes 1179648 | tf_op jit(solution)/shard_map/sub | solution.py:314
Async XLA Ops:
  0.6 52.8 %copy-start = (f32[32,3,1024]{2,0,1:T(8,128)S(1)}, f32[32,3,1024]{2,0,1:T(8,128)}, u32[]{:S(2)}) copy-start(f32[32,3,1024]{2,0,1:T(8,128)} %param.9) | copy-start | bytes 1179652

commit v4 on v0

v4 whole, which is shorter than its diff:
```python
import functools

import jax
import jax.numpy as jnp
from jax import lax
from jax.experimental import pallas as pl
from jax.experimental.pallas import tpu as pltpu
from jax.sharding import PartitionSpec as P

MESH = pl.DeviceIdType.MESH
F32 = jnp.float32
BF16 = jnp.bfloat16
NX, NY, NZ = 4, 4, 8
NC = 8
V = 24
W = 128
HALF = 512
LAG = 2
ORDER = (1, 7, 2, 6, 3, 5, 4)
SLOT = {0: 0, 6: 1, 2: 2, 4: 3, 7: 0, 1: 1, 5: 2, 3: 3}
EVEN = (0, 6, 2, 4)
ODD = (7, 1, 5, 3)
NP = 4
NT = (((1,), (1,)), ((), ()))


def split(value):
    high = value.astype(BF16)
    return high, (value - high.astype(F32)).astype(BF16)


def kernel(h_ref, d_ref, c_ref, f_ref, sol_ref, upd_ref,
           h_buf, d_buf, c_buf, f_buf, ft_hi, ft_lo, part, got, pair, own, sol_in, S, acc, M, R,
           h_sem, load_sem, fs, fr, a_ss, a_rs, b_ss, b_rs, m_ss, m_rs, z_ss, z_rs, y_ss, y_rs, e_ss, e_rs):
    row, col = lax.axis_index("row"), lax.axis_index("col")
    z, y = row // NY, row % NY
    x, k = col // 2, col % 2
    source = z % 2 == k
    other = z % 2 != k
    partner = (row, x * 2 + 1 - k)

    def place(zz, yy):
        return zz * NY + yy

    def remote(src, dst, ss, rs, to):
        return pltpu.make_async_remote_copy(
            src_ref=src, dst_ref=dst, send_sem=ss, recv_sem=rs, device_id=to, device_id_type=MESH)

    barrier = pltpu.get_barrier_semaphore()
    friends = [(row, (col + o) % NC) for o in range(1, NC)]
    friends += [(place(z, (y + dy) % NY), col) for dy in range(1, NY)]
    friends += [(place((z + dz) % NZ, y), col) for dz in range(1, NZ)]
    for dev in friends:
        pl.semaphore_signal(barrier, inc=1, device_id=dev, device_id_type=MESH)

    loads = [
        pltpu.make_async_copy(d_ref.at[0], d_buf.at[0], load_sem.at[0]),
        pltpu.make_async_copy(c_ref, c_buf, load_sem.at[1]),
        pltpu.make_async_copy(d_ref.at[1], d_buf.at[1], load_sem.at[2]),
    ]
    for p in range(2):
        loads.append(pltpu.make_async_copy(f_ref.at[:, p], f_buf.at[p, k], load_sem.at[3 + p]))
    heads = [
        pltpu.make_async_copy(h_ref.at[:, comp, p], h_buf.at[p, comp * 8:(comp + 1) * 8], h_sem.at[p, comp])
        for p in range(2) for comp in range(3)
    ]
    for load in heads + loads:
        load.start()

    def partial(stage, value, matrix):
        hi, lo = split(value)
        both = jnp.concatenate([hi, lo], axis=0)
        for b in range(NC):
            m_hi, m_lo = split(matrix[b * W:(b + 1) * W, :])
            one = lax.dot_general(both, m_hi, NT, preferred_element_type=F32)
            two = lax.dot_general(hi, m_lo, NT, preferred_element_type=F32)
            part[stage, b] = one[:V] + (one[V:] + two)

    def exchange(stage, o):
        to = (col + o) % NC
        return remote(part.at[stage, to], got.at[stage, o], a_ss.at[stage, o], a_rs.at[stage, o], (row, to))

    for load in heads:
        load.wait()
    loads[0].wait()
    partial(0, h_buf[0], d_buf.at[0])
    pl.semaphore_wait(barrier, len(friends))
    for o in range(1, NC):
        @pl.when(col + o < NC)
        def _():
            exchange(0, o).start()
    f_sends = [remote(f_ref.at[:, p], f_buf.at[p, k], fs.at[p], fr.at[p], partner) for p in range(2)]
    for copy in f_sends:
        copy.start()
    loads[1].wait()
    loads[2].wait()
    own[...] = part[0, col]
    for o in range(1, NC):
        @pl.when(col >= o)
        def _():
            exchange(0, o).wait_recv()
            own[...] = own[...] + got[0, o]
    first = own[...]
    sol_ref[0] = first
    partial(1, first, c_buf)
    for o in range(1, NC):
        exchange(1, o).start()

    def give(p):
        return remote(own, S.at[0, 0, y, k], m_ss.at[0], m_rs.at[0], partner)

    def share_z(p, dz):
        slot = SLOT[(NZ - dz) % NZ]
        there = (place((z + dz) % NZ, y), col)
        return remote(S.at[p, 0, y], S.at[p, slot, y], z_ss.at[p, dz], z_rs.at[p, slot], there)

    def wait_z(p, i):
        def wait():
            remote(S.at[p, 0, y], S.at[p, i, y], z_ss.at[p, 1], z_rs.at[p, i], partner).wait_recv()

        if i == 0:
            pl.when(other)(wait)
        else:
            wait()

    def share_y(p, i, dy):
        block = S.at[p, i, y] if p == 1 else S.at[p, :, y]
        there = (place(z, (y + dy) % NY), col)
        return remote(block, block, y_ss.at[p, i, dy], y_rs.at[p, i, dy], there)

    def start_y(p, i):
        for dy in range(1, NY):
            share_y(p, i, dy).start()

    @pl.when(other)
    def _():
        give(0).start()

    @pl.when(source)
    def _():
        S[0, 0, y, k] = first
        remote(own, S.at[0, 0, y, 1 - k], m_ss.at[0], m_rs.at[0], partner).wait_recv()
        for dz in ORDER:
            share_z(0, dz).start()

    def turn(p):
        loads[3 + p].wait()
        f_sends[p].wait_recv()
        for kk in range(2):
            hi, lo = split(f_buf[p, kk].T)
            ft_hi[p, kk * W:(kk + 1) * W, :] = hi
            ft_lo[p, kk * W:(kk + 1) * W, :] = lo

    turn(0)

    moved = part[1, col]
    for o in range(1, NC):
        exchange(1, o).wait_recv()
        moved = moved + got[1, o]
    partial(2, h_buf[1] - moved, d_buf.at[1])

    def deliver(o):
        to = (x + o) % NX
        return remote(part.at[2, pl.ds(to * 2, 2)], pair.at[o, k], b_ss.at[o], b_rs.at[o, k], (row, to * 2 + z % 2))

    def delivered(o, kk):
        return remote(part.at[2, pl.ds(x * 2, 2)], pair.at[o, kk], b_ss.at[o], b_rs.at[o, kk], partner)

    for o in range(1, NX):
        @pl.when(x + o < NX)
        def _():
            deliver(o).start()

    @pl.when(other)
    def _():
        deliver(0).start()

    for i in range(NP):
        wait_z(0, i)
    start_y(0, 0)
    turn(1)

    def reply():
        return remote(S.at[1, 0, y, 1 - k], sol_in, m_ss.at[1], m_rs.at[1], partner)

    @pl.when(source)
    def _():
        S[1, 0, y] = part[2, pl.ds(x * 2, 2)]
        for o in range(1, NX):
            @pl.when(x >= o)
            def _():
                for kk in range(2):
                    delivered(o, kk).wait_recv()
                S[1, 0, y] = S[1, 0, y] + (pair[o, 0] + pair[o, 1])

        delivered(0, 1 - k).wait_recv()
        S[1, 0, y] = S[1, 0, y] + pair[0, 1 - k]
        start_y(1, 0)
        for dz in ORDER:
            share_z(1, dz).start()
        reply().start()
        sol_ref[1] = S[1, 0, y, k]

    def update(p, i):
        s = jnp.concatenate([S[p, i, :, 0].reshape(4 * V, W), S[p, i, :, 1].reshape(4 * V, W)], axis=1)
        hi, lo = split(s)
        both = jnp.concatenate([hi, lo], axis=0)
        parts = []
        for half in range(2):
            at = slice(half * HALF, (half + 1) * HALF)
            one = jnp.dot(both, ft_hi[p, :, at], preferred_element_type=F32)
            two = jnp.dot(hi, ft_lo[p, :, at], preferred_element_type=F32)
            parts.append(one[:4 * V] + (one[4 * V:] + two))
        return parts

    right, left = (x + 1) % NX, (x + NX - 1) % NX

    def target(i):
        return (z + jnp.where(source, EVEN[i], ODD[i])) % NZ // 2

    def over(i, half):
        to = (left if half else right) * 2 + k
        return remote(acc.at[i, half], M.at[half], e_ss.at[0, half], e_rs.at[0, half], (row, to))

    def direct(i, half):
        to = (right if half else left) * 2 + k
        return remote(acc.at[i, half], R.at[0, half], e_ss.at[1, half], e_rs.at[1, half], (row, to))

    def merged(i, half):
        to = (left if half else right) * 2 + k
        return remote(acc.at[i, half], R.at[1, half], e_ss.at[2, half], e_rs.at[2, half], (row, to))

    def finish(i):
        for dy in range(1, NY):
            share_y(1, i, dy).wait_recv()
        for half, value in enumerate(update(1, i)):
            acc[i, half] = acc[i, half] + value
        to = target(i)

        @pl.when((to - x + NX) % NX == 2)
        def _():
            over(i, 0).start()
            over(i, 1).start()

        @pl.when(to == right)
        def _():
            direct(i, 1).start()

        @pl.when(to == left)
        def _():
            direct(i, 0).start()

    def merge(i):
        to = target(i)
        for half in range(2):
            @pl.when(to == (left if half else right))
            def _():
                over(i, half).wait_recv()
                acc[i, half] = acc[i, half] + M[half]
                merged(i, half).start()

    def forward(i):
        wait_z(1, i)
        if i == 0:
            @pl.when(other)
            def _():
                start_y(1, 0)
        else:
            start_y(1, i)

    def begin(i, carry):
        for half, value in enumerate(update(0, i)):
            acc[i, half] = value
        return carry

    for dy in range(1, NY):
        share_y(0, 0, dy).wait_recv()
    forward(0)
    forward(1)
    lax.fori_loop(0, NP, begin, 0)
    forward(2)
    finish(0)
    forward(3)
    for i in range(1, NP):
        finish(i)
        if i >= LAG:
            merge(i - LAG)
    for i in range(NP - LAG, NP):
        merge(i)

    mine = sum(jnp.where(target(i) == x, i, 0) for i in range(NP))
    for half in range(2):
        direct(0, half).wait_recv()
        merged(0, half).wait_recv()
        value = acc[mine, half] + (R[0, half] + R[1, half])
        for yy in range(NY):
            for comp in range(3):
                at = yy * V + comp * 8
                upd_ref[comp, yy * 8:(yy + 1) * 8, half * HALF:(half + 1) * HALF] = value[at:at + 8]

    @pl.when(other)
    def _():
        reply().wait_recv()
        sol_ref[1] = sol_in[...]

    for o in range(1, NC):
        @pl.when(col + o < NC)
        def _():
            exchange(0, o).wait_send()

        exchange(1, o).wait_send()
    for o in range(1, NX):
        @pl.when(x + o < NX)
        def _():
            deliver(o).wait_send()

    @pl.when(other)
    def _():
        deliver(0).wait_send()
        give(0).wait_send()

    @pl.when(source)
    def _():
        reply().wait_send()
        for p in range(2):
            for dz in ORDER:
                share_z(p, dz).wait_send()

    for dy in range(1, NY):
        share_y(0, 0, dy).wait_send()
        for i in range(NP):
            share_y(1, i, dy).wait_send()
    for copy in f_sends:
        copy.wait_send()
    for half in range(2):
        over(0, half).wait_send()
        direct(0, half).wait_send()
        merged(0, half).wait_send()


def body(head_deflections, diag_inverse, coupling, panel_factor, trailing):
    rows = panel_factor.shape[0]
    any_spec = pl.BlockSpec(memory_space=pl.ANY)
    vmem = pl.BlockSpec(memory_space=pltpu.VMEM)
    dma = pltpu.SemaphoreType.DMA
    solved, moved = pl.pallas_call(
        kernel,
        out_shape=(
            jax.ShapeDtypeStruct((2, V, W), F32),
            jax.ShapeDtypeStruct((3, 4 * 8, rows), F32),
        ),
        in_specs=[any_spec] * 4,
        out_specs=(vmem, vmem),
        scratch_shapes=[
            pltpu.VMEM((2, V, W), F32),
            pltpu.VMEM((2, 1024, W), F32),
            pltpu.VMEM((1024, W), F32),
            pltpu.VMEM((2, 2, rows, W), F32),
            pltpu.VMEM((2, 2 * W, rows), BF16),
            pltpu.VMEM((2, 2 * W, rows), BF16),
            pltpu.VMEM((3, NC, V, W), F32),
            pltpu.VMEM((2, NC, V, W), F32),
            pltpu.VMEM((NX, 2, 2, V, W), F32),
            pltpu.VMEM((V, W), F32),
            pltpu.VMEM((V, W), F32),
            pltpu.VMEM((2, NP, NY, 2, V, W), F32),
            pltpu.VMEM((NP, 2, 4 * V, HALF), F32),
            pltpu.VMEM((2, 4 * V, HALF), F32),
            pltpu.VMEM((2, 2, 4 * V, HALF), F32),
            dma((2, 3)), dma((5,)), dma((2,)), dma((2,)),
            dma((2, NC)), dma((2, NC)),
            dma((NX,)), dma((NX, 2)),
            dma((2,)), dma((2,)),
            dma((2, NZ)), dma((2, NP)),
            dma((2, NP, NY)), dma((2, NP, NY)),
            dma((3, 2)), dma((3, 2)),
        ],
        compiler_params=pltpu.CompilerParams(
            collective_id=0, has_side_effects=True, vmem_limit_bytes=60 << 20),
    )(head_deflections, diag_inverse, coupling, panel_factor)
    rest = trailing - jnp.transpose(moved, (1, 0, 2))
    out = jnp.transpose(solved.reshape(2, 3, 8, W), (2, 1, 0, 3))
    return (out, rest)


def solution(mesh):
    placed = (
        P("row", None, None, "col"),
        P(None, None, "col"),
        P(None, "col"),
        P("row", None, "col"),
        P("col", None, "row"),
    )
    return jax.shard_map(
        body,
        mesh=mesh,
        in_specs=placed,
        out_specs=(P("row", None, None, "col"), P("col", None, "row")),
        check_vma=False,
    )
```

time: 219 us -> 51 us (0.23); the launches traced: 215 us -> 50.7 us
  waiting for transfers between devices: 92.3 us -> 0 us
  blocking collectives: 87.8 us -> 0 us
  Pallas kernels: 0 us -> 46.9 us
  matrix products: 14.5 us -> 0 us
  between operations: 13.8 us -> 0.65 us
  local copies, waits for them, and re-layouts: 4.08 us -> 1.36 us
    reduce_scatter x5 -> x0, waiting for transfers between devices: 92.2 us -> none  [the longest x2 34.2 us: panel_update(): lax.psum_scatter(panel_terms(solved_all, factor), 'col', scatter_dimensio...]
    all_gather x2 -> x0, blocking collectives: 87.8 us -> none  [share_steps(): return lax.all_gather(solved_own, 'row', axis=0, tiled=True)]
    pallas_call x0 -> x1, Pallas kernels: none -> 46.9 us  [body(): pl.pallas_call(kernel, out_shape=(jax.ShapeDtypeStruct((2, V, W), F32), j...]
    dot_general x5 -> x0, matrix products: 14.5 us -> none  [the longest x2 8.56 us: panel_terms(): lax.dot_general(solved_all, factor, (((2,), (1,)), ((), ())), precision=l...]
    slice x2 -> x0, local copies, waits for them, and re-layouts: 3.43 us -> none  [the longest x1 2.54 us: body(): first_update = panel_update(first_all, panel_factor[:, 0, :])]
  transfers between devices with their start and end apart: 5 -> 0, of which waited for: 3 -> 0; matrix products, arithmetic and copies ran while one was open for 5% -> 0% of each run, Pallas kernels for 0% -> 0%
where the time goes in v4:
time: 51 us; the launch traced here: 50.7 us
  Pallas kernels  46.9 us (92%)
  other arithmetic  1.78 us (3%)
  local copies, waits for them, and re-layouts  1.36 us (3%)
  between operations  0.65 us (1%)
    pallas_call x1, Pallas kernels, body(): pl.pallas_call(kernel, out_shape=(jax.ShapeDtypeStruct((2, V, W), F32), j...  46.9 us
    sub x1, other arithmetic, body(): rest = trailing - jnp.transpose(moved, (1, 0, 2))  1.78 us
    reshape x1, local copies, waits for them, and re-layouts, body(): out = jnp.transpose(solved.reshape(2, 3, 8, W), (2, 1, 0, 3))  1.36 us

profile of v4, /device:TPU:38, one launch (start us, length us, event | category | flops | bytes accessed | tf_op | source)
XLA Modules:
  0.0 50.7 jit_solution(1570908356077566556)
XLA Ops:
  0.6 0.0 copy-start
  0.6 46.9 %shard_map.68 = (f32[2,24,128]{2,1,0:T(8,128)}, f32[3,32,1024]{2,1,0:T(8,128)}) custom-call(f32[8,3,2,128]{3,2,1,0:T(2,128)} %h_ref.1, f32[2,1024,128]{2,1,0:T(8,128)} %d_ref.1, f32[1024,128]{1,0:T(8,128)} %c_ref.1, f32[1024,2,128]{2,1,0:T(2,128)} %f_ref.1), custom_call_target="tpu_custom_call" | custom-call | tf_op jit(solution)/shard_map/pallas_call | solution.py:346
  47.6 1.4 %copy.9 = f32[2,3,8,128]{3,0,1,2:T(2,128)} copy(f32[2,3,8,128]{3,2,1,0:T(8,128)} %bitcast.7) | data formatting | bytes 49152 | tf_op jit(solution)/shard_map/reshape | solution.py:382
  48.9 0.0 copy-done
  48.9 1.8 %bitcast_subtract_fusion = f32[32,3,1024]{2,0,1:T(8,128)} fusion(f32[32,3,1024]{2,0,1:T(8,128)S(1)} %copy-done, f32[3,32,1024]{2,1,0:T(8,128)} %get-tuple-element.5), kind=kLoop, calls=%fused_computation | loop fusion | flops 98304 | bytes 1179648 | tf_op jit(solution)/shard_map/sub | solution.py:381
Async XLA Ops:
  0.6 48.3 %copy-start = (f32[32,3,1024]{2,0,1:T(8,128)S(1)}, f32[32,3,1024]{2,0,1:T(8,128)}, u32[]{:S(2)}) copy-start(f32[32,3,1024]{2,0,1:T(8,128)} %param.9) | copy-start | bytes 1179652

commit v5 on v4

--- a/solution.py
+++ b/solution.py
@@ -15,7 +15,9 @@
 V = 24
 W = 128
 HALF = 512
-LAG = 2
+LAG = 3
+PIECES = 2
+ROWS = 4 * V // PIECES
 ORDER = (1, 7, 2, 6, 3, 5, 4)
 SLOT = {0: 0, 6: 1, 2: 2, 4: 3, 7: 0, 1: 1, 5: 2, 3: 3}
 EVEN = (0, 6, 2, 4)
@@ -30,8 +32,8 @@
 
 
 def kernel(h_ref, d_ref, c_ref, f_ref, sol_ref, upd_ref,
-           h_buf, d_buf, c_buf, f_buf, ft_hi, ft_lo, part, got, pair, own, sol_in, S, acc, M, R,
-           h_sem, load_sem, fs, fr, a_ss, a_rs, b_ss, b_rs, m_ss, m_rs, z_ss, z_rs, y_ss, y_rs, e_ss, e_rs):
+           h_buf, d_buf, c_buf, f_buf, f_turn, ft_hi, ft_lo, part, got, pair, own, sol_in, S, acc, M, R,
+           h_sem, load_sem, fs, fr, a_ss, a_rs, b_ss, b_rs, m_ss, m_rs, z_ss, z_rs, y_ss, y_rs, e_ss, e_rs, o_ss, o_rs):
     row, col = lax.axis_index("row"), lax.axis_index("col")
     z, y = row // NY, row % NY
     x, k = col // 2, col % 2
@@ -46,26 +48,26 @@
         return pltpu.make_async_remote_copy(
             src_ref=src, dst_ref=dst, send_sem=ss, recv_sem=rs, device_id=to, device_id_type=MESH)
 
+    loads = [
+        pltpu.make_async_copy(d_ref.at[0], d_buf.at[0], load_sem.at[0]),
+        pltpu.make_async_copy(c_ref, c_buf, load_sem.at[1]),
+        pltpu.make_async_copy(d_ref.at[1], d_buf.at[1], load_sem.at[2]),
+    ]
+    for p in range(2):
+        loads.append(pltpu.make_async_copy(f_ref.at[:, p], f_buf.at[p], load_sem.at[3 + p]))
+    heads = [
+        pltpu.make_async_copy(h_ref.at[:, comp, p], h_buf.at[p, comp * 8:(comp + 1) * 8], h_sem.at[p, comp])
+        for p in range(2) for comp in range(3)
+    ]
+    for load in heads + loads:
+        load.start()
+
     barrier = pltpu.get_barrier_semaphore()
     friends = [(row, (col + o) % NC) for o in range(1, NC)]
     friends += [(place(z, (y + dy) % NY), col) for dy in range(1, NY)]
     friends += [(place((z + dz) % NZ, y), col) for dz in range(1, NZ)]
     for dev in friends:
         pl.semaphore_signal(barrier, inc=1, device_id=dev, device_id_type=MESH)
-
-    loads = [
-        pltpu.make_async_copy(d_ref.at[0], d_buf.at[0], load_sem.at[0]),
-        pltpu.make_async_copy(c_ref, c_buf, load_sem.at[1]),
-        pltpu.make_async_copy(d_ref.at[1], d_buf.at[1], load_sem.at[2]),
-    ]
-    for p in range(2):
-        loads.append(pltpu.make_async_copy(f_ref.at[:, p], f_buf.at[p, k], load_sem.at[3 + p]))
-    heads = [
-        pltpu.make_async_copy(h_ref.at[:, comp, p], h_buf.at[p, comp * 8:(comp + 1) * 8], h_sem.at[p, comp])
-        for p in range(2) for comp in range(3)
-    ]
-    for load in heads + loads:
-        load.start()
 
     def partial(stage, value, matrix):
         hi, lo = split(value)
@@ -84,12 +86,15 @@
         load.wait()
     loads[0].wait()
     partial(0, h_buf[0], d_buf.at[0])
+    for p in range(2):
+        loads[3 + p].wait()
+        f_turn[p, k] = f_buf[p].T
     pl.semaphore_wait(barrier, len(friends))
     for o in range(1, NC):
         @pl.when(col + o < NC)
         def _():
             exchange(0, o).start()
-    f_sends = [remote(f_ref.at[:, p], f_buf.at[p, k], fs.at[p], fr.at[p], partner) for p in range(2)]
+    f_sends = [remote(f_turn.at[p, k], f_turn.at[p, k], fs.at[p], fr.at[p], partner) for p in range(2)]
     for copy in f_sends:
         copy.start()
     loads[1].wait()
@@ -144,10 +149,9 @@
             share_z(0, dz).start()
 
     def turn(p):
-        loads[3 + p].wait()
         f_sends[p].wait_recv()
         for kk in range(2):
-            hi, lo = split(f_buf[p, kk].T)
+            hi, lo = split(f_turn[p, kk])
             ft_hi[p, kk * W:(kk + 1) * W, :] = hi
             ft_lo[p, kk * W:(kk + 1) * W, :] = lo
 
@@ -218,17 +222,22 @@
     def target(i):
         return (z + jnp.where(source, EVEN[i], ODD[i])) % NZ // 2
 
-    def over(i, half):
+    def piece(n):
+        return pl.ds(n * ROWS, ROWS)
+
+    def over(i, half, n):
         to = (left if half else right) * 2 + k
-        return remote(acc.at[i, half], M.at[half], e_ss.at[0, half], e_rs.at[0, half], (row, to))
+        return remote(acc.at[i, half, piece(n)], M.at[half, piece(n)],
+                      o_ss.at[0, half, n], o_rs.at[0, half, n], (row, to))
 
     def direct(i, half):
         to = (right if half else left) * 2 + k
-        return remote(acc.at[i, half], R.at[0, half], e_ss.at[1, half], e_rs.at[1, half], (row, to))
-
-    def merged(i, half):
+        return remote(acc.at[i, half], R.at[0, half], e_ss.at[half], e_rs.at[half], (row, to))
+
+    def merged(i, half, n):
         to = (left if half else right) * 2 + k
-        return remote(acc.at[i, half], R.at[1, half], e_ss.at[2, half], e_rs.at[2, half], (row, to))
+        return remote(acc.at[i, half, piece(n)], R.at[1, half, piece(n)],
+                      o_ss.at[1, half, n], o_rs.at[1, half, n], (row, to))
 
     def finish(i):
         for dy in range(1, NY):
@@ -239,8 +248,9 @@
 
         @pl.when((to - x + NX) % NX == 2)
         def _():
-            over(i, 0).start()
-            over(i, 1).start()
+            for n in range(PIECES):
+                over(i, 0, n).start()
+                over(i, 1, n).start()
 
         @pl.when(to == right)
         def _():
@@ -255,9 +265,10 @@
         for half in range(2):
             @pl.when(to == (left if half else right))
             def _():
-                over(i, half).wait_recv()
-                acc[i, half] = acc[i, half] + M[half]
-                merged(i, half).start()
+                for n in range(PIECES):
+                    over(i, half, n).wait_recv()
+                    acc[i, half, piece(n)] = acc[i, half, piece(n)] + M[half, piece(n)]
+                    merged(i, half, n).start()
 
     def forward(i):
         wait_z(1, i)
@@ -268,20 +279,20 @@
         else:
             start_y(1, i)
 
-    def begin(i, carry):
+    def begin(i):
         for half, value in enumerate(update(0, i)):
             acc[i, half] = value
-        return carry
 
     for dy in range(1, NY):
         share_y(0, 0, dy).wait_recv()
     forward(0)
     forward(1)
-    lax.fori_loop(0, NP, begin, 0)
+    begin(0)
     forward(2)
-    finish(0)
     forward(3)
-    for i in range(1, NP):
+    for i in range(NP):
+        if i > 0:
+            begin(i)
         finish(i)
         if i >= LAG:
             merge(i - LAG)
@@ -291,12 +302,14 @@
     mine = sum(jnp.where(target(i) == x, i, 0) for i in range(NP))
     for half in range(2):
         direct(0, half).wait_recv()
-        merged(0, half).wait_recv()
-        value = acc[mine, half] + (R[0, half] + R[1, half])
-        for yy in range(NY):
-            for comp in range(3):
-                at = yy * V + comp * 8
-                upd_ref[comp, yy * 8:(yy + 1) * 8, half * HALF:(half + 1) * HALF] = value[at:at + 8]
+    for n in range(PIECES):
+        for half in range(2):
+            merged(0, half, n).wait_recv()
+            for unit in range(n * ROWS // 8, (n + 1) * ROWS // 8):
+                yy, comp = unit // 3, unit % 3
+                rows = slice(unit * 8, unit * 8 + 8)
+                value = acc[mine, half, rows] + (R[0, half, rows] + R[1, half, rows])
+                upd_ref[comp, yy * 8:(yy + 1) * 8, half * HALF:(half + 1) * HALF] = value
 
     @pl.when(other)
     def _():
@@ -333,9 +346,10 @@
     for copy in f_sends:
         copy.wait_send()
     for half in range(2):
-        over(0, half).wait_send()
         direct(0, half).wait_send()
-        merged(0, half).wait_send()
+        for n in range(PIECES):
+            over(0, half, n).wait_send()
+            merged(0, half, n).wait_send()
 
 
 def body(head_deflections, diag_inverse, coupling, panel_factor, trailing):
@@ -355,7 +369,8 @@
             pltpu.VMEM((2, V, W), F32),
             pltpu.VMEM((2, 1024, W), F32),
             pltpu.VMEM((1024, W), F32),
-            pltpu.VMEM((2, 2, rows, W), F32),
+            pltpu.VMEM((2, rows, W), F32),
+            pltpu.VMEM((2, 2, W, rows), F32),
             pltpu.VMEM((2, 2 * W, rows), BF16),
             pltpu.VMEM((2, 2 * W, rows), BF16),
             pltpu.VMEM((3, NC, V, W), F32),
@@ -373,10 +388,11 @@
             dma((2,)), dma((2,)),
             dma((2, NZ)), dma((2, NP)),
             dma((2, NP, NY)), dma((2, NP, NY)),
-            dma((3, 2)), dma((3, 2)),
+            dma((2,)), dma((2,)),
+            dma((2, 2, PIECES)), dma((2, 2, PIECES)),
         ],
         compiler_params=pltpu.CompilerParams(
-            collective_id=0, has_side_effects=True, vmem_limit_bytes=60 << 20),
+            collective_id=0, has_side_effects=True, vmem_limit_bytes=int(53.5 * (1 << 20))),
     )(head_deflections, diag_inverse, coupling, panel_factor)
     rest = trailing - jnp.transpose(moved, (1, 0, 2))
     out = jnp.transpose(solved.reshape(2, 3, 8, W), (2, 1, 0, 3))

time: 51 us -> 47.8 us (0.937)
  Pallas kernels: 46.9 us -> 44.9 us
  other arithmetic: 1.78 us -> 0.79 us
    pallas_call x1, Pallas kernels: 46.9 us -> 44.9 us  [body(): pl.pallas_call(kernel, out_shape=(jax.ShapeDtypeStruct((2, V, W), F32), j...]
    sub x1, other arithmetic: 1.78 us -> 0.79 us  [body(): rest = trailing - jnp.transpose(moved, (1, 0, 2))]
    reshape x1, local copies, waits for them, and re-layouts: 1.36 us -> 0.62 us  [body(): out = jnp.transpose(solved.reshape(2, 3, 8, W), (2, 1, 0, 3))]
    unnamed x2 -> x4, local copies, waits for them, and re-layouts: 0.01 us -> 0.73 us
where the time goes in v5:
time: 47.8 us; the launch traced here: 47.7 us
  Pallas kernels  44.9 us (94%)
  local copies, waits for them, and re-layouts  1.36 us (3%)
  other arithmetic  0.79 us (2%)
  between operations  0.65 us (1%)
    pallas_call x1, Pallas kernels, body(): pl.pallas_call(kernel, out_shape=(jax.ShapeDtypeStruct((2, V, W), F32), j...  44.9 us

profile of v5, /device:TPU:38, one launch (start us, length us, event | category | flops | bytes accessed | tf_op | source)
XLA Modules:
  0.0 47.7 jit_solution(15106874371579265672)
XLA Ops:
  0.6 0.0 copy-start
  0.6 0.7 %copy-done = f32[8,3,2,128]{3,2,1,0:T(2,128)S(1)} copy-done((f32[8,3,2,128]{3,2,1,0:T(2,128)S(1)}, f32[8,3,2,128]{3,2,1,0:T(2,128)}, u32[]{:S(2)}) %copy-start) | copy-done | bytes 24600
  1.4 0.0 copy-start.1
  1.4 44.9 %shard_map.68 = (f32[2,24,128]{2,1,0:T(8,128)S(1)}, f32[3,32,1024]{2,1,0:T(8,128)S(1)}) custom-call(f32[8,3,2,128]{3,2,1,0:T(2,128)S(1)} %copy-done, f32[2,1024,128]{2,1,0:T(8,128)} %d_ref.1, f32[1024,128]{1,0:T(8,128)} %c_ref.1, f32[1024,2,128]{2,1,0:T(2,128)} %f_ref.1), custom_call_target="tpu_custom_call" | custom-call | tf_op jit(solution)/shard_map/pallas_call | solution.py:360
  46.3 0.6 %copy.9 = f32[2,3,8,128]{3,0,1,2:T(2,128)} copy(f32[2,3,8,128]{3,2,1,0:T(8,128)S(1)} %bitcast.6) | data formatting | bytes 49152 | tf_op jit(solution)/shard_map/reshape | solution.py:398
  46.9 0.0 copy-done.1
  46.9 0.8 %bitcast_subtract_fusion = f32[32,3,1024]{2,0,1:T(8,128)} fusion(f32[32,3,1024]{2,0,1:T(8,128)S(1)} %copy-done.1, f32[3,32,1024]{2,1,0:T(8,128)S(1)} %get-tuple-element.5), kind=kLoop, calls=%fused_computation | loop fusion | flops 98304 | bytes 1179648 | tf_op jit(solution)/shard_map/sub | solution.py:397
Async XLA Ops:
  0.6 0.7 %copy-start = (f32[8,3,2,128]{3,2,1,0:T(2,128)S(1)}, f32[8,3,2,128]{3,2,1,0:T(2,128)}, u32[]{:S(2)}) copy-start(f32[8,3,2,128]{3,2,1,0:T(2,128)} %h_ref.1) | copy-start | bytes 73732
  1.4 45.5 %copy-start.1 = (f32[32,3,1024]{2,0,1:T(8,128)S(1)}, f32[32,3,1024]{2,0,1:T(8,128)}, u32[]{:S(2)}) copy-start(f32[32,3,1024]{2,0,1:T(8,128)} %param.9) | copy-start | bytes 1179652

commit v6 on v5

--- a/solution.py
+++ b/solution.py
@@ -283,16 +283,13 @@
         for half, value in enumerate(update(0, i)):
             acc[i, half] = value
 
+    for i in range(NP):
+        forward(i)
     for dy in range(1, NY):
         share_y(0, 0, dy).wait_recv()
-    forward(0)
-    forward(1)
-    begin(0)
-    forward(2)
-    forward(3)
     for i in range(NP):
-        if i > 0:
-            begin(i)
+        begin(i)
+    for i in range(NP):
         finish(i)
         if i >= LAG:
             merge(i - LAG)

time: 47.8 us -> 46.9 us (0.981)
  Pallas kernels: 44.9 us -> 43.8 us
    pallas_call x1, Pallas kernels: 44.9 us -> 43.8 us  [body(): pl.pallas_call(kernel, out_shape=(jax.ShapeDtypeStruct((2, V, W), F32), j...]
where the time goes in v6:
time: 46.9 us; the launch traced here: 46.6 us
  Pallas kernels  43.8 us (93%)
  local copies, waits for them, and re-layouts  1.36 us (3%)
  other arithmetic  0.79 us (2%)
  between operations  0.65 us (1%)
    pallas_call x1, Pallas kernels, body(): pl.pallas_call(kernel, out_shape=(jax.ShapeDtypeStruct((2, V, W), F32), j...  43.8 us

profile of v6, /device:TPU:38, one launch (start us, length us, event | category | flops | bytes accessed | tf_op | source)
XLA Modules:
  0.0 46.6 jit_solution(5801037306040764114)
XLA Ops:
  0.6 0.0 copy-start
  0.6 0.7 %copy-done = f32[8,3,2,128]{3,2,1,0:T(2,128)S(1)} copy-done((f32[8,3,2,128]{3,2,1,0:T(2,128)S(1)}, f32[8,3,2,128]{3,2,1,0:T(2,128)}, u32[]{:S(2)}) %copy-start) | copy-done | bytes 24600
  1.4 0.0 copy-start.1
  1.4 43.8 %shard_map.68 = (f32[2,24,128]{2,1,0:T(8,128)S(1)}, f32[3,32,1024]{2,1,0:T(8,128)S(1)}) custom-call(f32[8,3,2,128]{3,2,1,0:T(2,128)S(1)} %copy-done, f32[2,1024,128]{2,1,0:T(8,128)} %d_ref.1, f32[1024,128]{1,0:T(8,128)} %c_ref.1, f32[1024,2,128]{2,1,0:T(2,128)} %f_ref.1), custom_call_target="tpu_custom_call" | custom-call | tf_op jit(solution)/shard_map/pallas_call | solution.py:357
  45.2 0.6 %copy.9 = f32[2,3,8,128]{3,0,1,2:T(2,128)} copy(f32[2,3,8,128]{3,2,1,0:T(8,128)S(1)} %bitcast.6) | data formatting | bytes 49152 | tf_op jit(solution)/shard_map/reshape | solution.py:395
  45.8 0.0 copy-done.1
  45.9 0.8 %bitcast_subtract_fusion = f32[32,3,1024]{2,0,1:T(8,128)} fusion(f32[32,3,1024]{2,0,1:T(8,128)S(1)} %copy-done.1, f32[3,32,1024]{2,1,0:T(8,128)S(1)} %get-tuple-element.5), kind=kLoop, calls=%fused_computation | loop fusion | flops 98304 | bytes 1179648 | tf_op jit(solution)/shard_map/sub | solution.py:394
Async XLA Ops:
  0.6 0.7 %copy-start = (f32[8,3,2,128]{3,2,1,0:T(2,128)S(1)}, f32[8,3,2,128]{3,2,1,0:T(2,128)}, u32[]{:S(2)}) copy-start(f32[8,3,2,128]{3,2,1,0:T(2,128)} %h_ref.1) | copy-start | bytes 73732
  1.4 44.5 %copy-start.1 = (f32[32,3,1024]{2,0,1:T(8,128)S(1)}, f32[32,3,1024]{2,0,1:T(8,128)}, u32[]{:S(2)}) copy-start(f32[32,3,1024]{2,0,1:T(8,128)} %param.9) | copy-start | bytes 1179652

commit v7 on v6

--- a/solution.py
+++ b/solution.py
@@ -65,9 +65,13 @@
     barrier = pltpu.get_barrier_semaphore()
     friends = [(row, (col + o) % NC) for o in range(1, NC)]
     friends += [(place(z, (y + dy) % NY), col) for dy in range(1, NY)]
-    friends += [(place((z + dz) % NZ, y), col) for dz in range(1, NZ)]
     for dev in friends:
         pl.semaphore_signal(barrier, inc=1, device_id=dev, device_id_type=MESH)
+    for dz in (2, 4, 6, 1, 3, 5, 7):
+        @pl.when(source if dz % 2 == 0 else other)
+        def _():
+            there = (place((z + dz) % NZ, y), col)
+            pl.semaphore_signal(barrier, inc=1, device_id=there, device_id_type=MESH)
 
     def partial(stage, value, matrix):
         hi, lo = split(value)
@@ -86,14 +90,14 @@
         load.wait()
     loads[0].wait()
     partial(0, h_buf[0], d_buf.at[0])
+    pl.semaphore_wait(barrier, len(friends) + jnp.where(source, NZ - 1, 0))
+    for o in range(1, NC):
+        @pl.when(col + o < NC)
+        def _():
+            exchange(0, o).start()
     for p in range(2):
         loads[3 + p].wait()
         f_turn[p, k] = f_buf[p].T
-    pl.semaphore_wait(barrier, len(friends))
-    for o in range(1, NC):
-        @pl.when(col + o < NC)
-        def _():
-            exchange(0, o).start()
     f_sends = [remote(f_turn.at[p, k], f_turn.at[p, k], fs.at[p], fr.at[p], partner) for p in range(2)]
     for copy in f_sends:
         copy.start()

time: 46.9 us -> 46.8 us (level)
  no operation moved by 1% of the time
where the time goes in v7:
time: 46.8 us; the launch traced here: 46.6 us
  Pallas kernels  43.8 us (94%)
  local copies, waits for them, and re-layouts  1.36 us (3%)
  other arithmetic  0.79 us (2%)
  between operations  0.65 us (1%)
    pallas_call x1, Pallas kernels, body(): pl.pallas_call(kernel, out_shape=(jax.ShapeDtypeStruct((2, V, W), F32), j...  43.8 us

profile of v7, /device:TPU:38, one launch (start us, length us, event | category | flops | bytes accessed | tf_op | source)
XLA Modules:
  0.0 46.6 jit_solution(15478269213520385164)
XLA Ops:
  0.6 0.0 copy-start
  0.6 0.7 %copy-done = f32[8,3,2,128]{3,2,1,0:T(2,128)S(1)} copy-done((f32[8,3,2,128]{3,2,1,0:T(2,128)S(1)}, f32[8,3,2,128]{3,2,1,0:T(2,128)}, u32[]{:S(2)}) %copy-start) | copy-done | bytes 24600
  1.4 0.0 copy-start.1
  1.4 43.8 %shard_map.68 = (f32[2,24,128]{2,1,0:T(8,128)S(1)}, f32[3,32,1024]{2,1,0:T(8,128)S(1)}) custom-call(f32[8,3,2,128]{3,2,1,0:T(2,128)S(1)} %copy-done, f32[2,1024,128]{2,1,0:T(8,128)} %d_ref.1, f32[1024,128]{1,0:T(8,128)} %c_ref.1, f32[1024,2,128]{2,1,0:T(2,128)} %f_ref.1), custom_call_target="tpu_custom_call" | custom-call | tf_op jit(solution)/shard_map/pallas_call | solution.py:361
  45.2 0.6 %copy.9 = f32[2,3,8,128]{3,0,1,2:T(2,128)} copy(f32[2,3,8,128]{3,2,1,0:T(8,128)S(1)} %bitcast.6) | data formatting | bytes 49152 | tf_op jit(solution)/shard_map/reshape | solution.py:399
  45.8 0.0 copy-done.1
  45.8 0.8 %bitcast_subtract_fusion = f32[32,3,1024]{2,0,1:T(8,128)} fusion(f32[32,3,1024]{2,0,1:T(8,128)S(1)} %copy-done.1, f32[3,32,1024]{2,1,0:T(8,128)S(1)} %get-tuple-element.5), kind=kLoop, calls=%fused_computation | loop fusion | flops 98304 | bytes 1179648 | tf_op jit(solution)/shard_map/sub | solution.py:398
Async XLA Ops:
  0.6 0.7 %copy-start = (f32[8,3,2,128]{3,2,1,0:T(2,128)S(1)}, f32[8,3,2,128]{3,2,1,0:T(2,128)}, u32[]{:S(2)}) copy-start(f32[8,3,2,128]{3,2,1,0:T(2,128)} %h_ref.1) | copy-start | bytes 73732
  1.4 44.5 %copy-start.1 = (f32[32,3,1024]{2,0,1:T(8,128)S(1)}, f32[32,3,1024]{2,0,1:T(8,128)}, u32[]{:S(2)}) copy-start(f32[32,3,1024]{2,0,1:T(8,128)} %param.9) | copy-start | bytes 1179652

commit v8 on v7

--- a/solution.py
+++ b/solution.py
@@ -16,7 +16,7 @@
 W = 128
 HALF = 512
 LAG = 3
-PIECES = 2
+PIECES = 3
 ROWS = 4 * V // PIECES
 ORDER = (1, 7, 2, 6, 3, 5, 4)
 SLOT = {0: 0, 6: 1, 2: 2, 4: 3, 7: 0, 1: 1, 5: 2, 3: 3}

time: 46.8 us -> 46.9 us (level)
  no operation moved by 1% of the time
where the time goes in v8:
time: 46.9 us; the launch traced here: 46.7 us
  Pallas kernels  43.9 us (94%)
  local copies, waits for them, and re-layouts  1.36 us (3%)
  other arithmetic  0.79 us (2%)
  between operations  0.65 us (1%)
    pallas_call x1, Pallas kernels, body(): pl.pallas_call(kernel, out_shape=(jax.ShapeDtypeStruct((2, V, W), F32), j...  43.9 us

profile of v8, /device:TPU:38, one launch (start us, length us, event | category | flops | bytes accessed | tf_op | source)
XLA Modules:
  0.0 46.7 jit_solution(11158854736955550996)
XLA Ops:
  0.6 0.0 copy-start
  0.6 0.7 %copy-done = f32[8,3,2,128]{3,2,1,0:T(2,128)S(1)} copy-done((f32[8,3,2,128]{3,2,1,0:T(2,128)S(1)}, f32[8,3,2,128]{3,2,1,0:T(2,128)}, u32[]{:S(2)}) %copy-start) | copy-done | bytes 24600
  1.4 0.0 copy-start.1
  1.4 43.9 %shard_map.68 = (f32[2,24,128]{2,1,0:T(8,128)S(1)}, f32[3,32,1024]{2,1,0:T(8,128)S(1)}) custom-call(f32[8,3,2,128]{3,2,1,0:T(2,128)S(1)} %copy-done, f32[2,1024,128]{2,1,0:T(8,128)} %d_ref.1, f32[1024,128]{1,0:T(8,128)} %c_ref.1, f32[1024,2,128]{2,1,0:T(2,128)} %f_ref.1), custom_call_target="tpu_custom_call" | custom-call | tf_op jit(solution)/shard_map/pallas_call | solution.py:361
  45.3 0.6 %copy.9 = f32[2,3,8,128]{3,0,1,2:T(2,128)} copy(f32[2,3,8,128]{3,2,1,0:T(8,128)S(1)} %bitcast.6) | data formatting | bytes 49152 | tf_op jit(solution)/shard_map/reshape | solution.py:399
  45.9 0.0 copy-done.1
  45.9 0.8 %bitcast_subtract_fusion = f32[32,3,1024]{2,0,1:T(8,128)} fusion(f32[32,3,1024]{2,0,1:T(8,128)S(1)} %copy-done.1, f32[3,32,1024]{2,1,0:T(8,128)S(1)} %get-tuple-element.5), kind=kLoop, calls=%fused_computation | loop fusion | flops 98304 | bytes 1179648 | tf_op jit(solution)/shard_map/sub | solution.py:398
Async XLA Ops:
  0.6 0.7 %copy-start = (f32[8,3,2,128]{3,2,1,0:T(2,128)S(1)}, f32[8,3,2,128]{3,2,1,0:T(2,128)}, u32[]{:S(2)}) copy-start(f32[8,3,2,128]{3,2,1,0:T(2,128)} %h_ref.1) | copy-start | bytes 73732
  1.4 44.5 %copy-start.1 = (f32[32,3,1024]{2,0,1:T(8,128)S(1)}, f32[32,3,1024]{2,0,1:T(8,128)}, u32[]{:S(2)}) copy-start(f32[32,3,1024]{2,0,1:T(8,128)} %param.9) | copy-start | bytes 1179652
